TPU v7x, 256 devices: a whole 4x4x8 slice. The times are simulated.
256 devices in a mesh: expert: 64 (over x, y_lo, z), dp: 4 (over y_hi, core).
Axes of the slice: x: 4, y: 4 (y_hi: 2, y_lo: 2; y = y_hi * 2 + y_lo), z: 8, core: 2. Of those that a mesh axis runs over, the one named last changes fastest.
Arguments:
- tokens: bfloat16 [256, 512, 1024], P(('expert', 'dp')), may hold values from -24 to 24
- slot_param: bfloat16 [1024, 64], replicated, may hold values from -2 to 2
- up_weight: bfloat16 [64, 1024, 4096], P('expert', None, 'dp'), may hold values from -0.1875 to 0.1875
- down_weight: bfloat16 [64, 4096, 1024], P('expert', 'dp'), may hold values from -0.09375 to 0.09375
- grad_output: bfloat16 [256, 512, 1024], P(('expert', 'dp')), may hold values from -6 to 6
Outputs:
- grad_tokens: bfloat16 [256, 512, 1024], P(('expert', 'dp'))
- grad_slot_param: float32 [1024, 64], replicated
- grad_up: bfloat16 [64, 1024, 4096], P('expert', None, 'dp')
- grad_down: bfloat16 [64, 4096, 1024], P('expert', 'dp')
All inputs are finite; a program needn't handle non-finite values.
Results may differ from a plain program's by a relative error of at most 0.013.
Values may be sent and summed in bfloat16 or wider, within the bound.
No kernel may reach another device: no remote copies, remote signals or barrier semaphores. Data moves between devices by JAX's collectives and lax.ppermute only.
A program may use at most 64 MiB of HBM per device.

v0:
```python
import jax
import jax.numpy as jnp
from jax import lax
from jax.sharding import PartitionSpec as P

gelu_coeff = 0.7978845608
cubic_coeff = 0.044715


def gelu_tanh(values):
    inner = gelu_coeff * (values + cubic_coeff * values * values * values)
    return 0.5 * values * (1.0 + jnp.tanh(inner))


def gelu_slope(values):
    inner = gelu_coeff * (values + cubic_coeff * values * values * values)
    tangent = jnp.tanh(inner)
    return 0.5 * (1.0 + tangent) + 0.5 * values * (1.0 - tangent * tangent) * gelu_coeff * (
        1.0 + 3.0 * cubic_coeff * values * values
    )


def shards(tokens, slot_param, up_weight, down_weight, grad_output):
    image_tokens = tokens[0]
    image_grads = grad_output[0]
    groups = lax.axis_size("expert")
    experts_here = up_weight.shape[0]
    slots = slot_param.shape[1]
    width = tokens.shape[2]
    over_rows = (((0,), (0,)), ((), ()))
    over_cols = (((1,), (1,)), ((), ()))
    logits = jnp.dot(image_tokens, slot_param, preferred_element_type=jnp.float32)
    dispatch = jax.nn.softmax(logits, axis=0)
    combine = jax.nn.softmax(logits, axis=1)
    dispatch_b = dispatch.astype(jnp.bfloat16)
    combine_b = combine.astype(jnp.bfloat16)
    slot_input = lax.dot_general(
        dispatch_b, image_tokens, over_rows, preferred_element_type=jnp.float32
    ).astype(jnp.bfloat16)
    slot_grad = lax.dot_general(
        combine_b, image_grads, over_rows, preferred_element_type=jnp.float32
    ).astype(jnp.bfloat16)

    def to_blocks(rows):
        return rows.reshape(1, groups, experts_here, width)

    def send_rows(blocks):
        moved_rows = lax.all_to_all(blocks, "expert", split_axis=1, concat_axis=1, tiled=True)
        return lax.all_gather(moved_rows, "dp", axis=0, tiled=True)

    def return_rows(partial_rows):
        summed_rows = lax.psum_scatter(partial_rows, "dp", scatter_dimension=0, tiled=True)
        moved_back = lax.all_to_all(
            summed_rows.astype(jnp.bfloat16), "expert", split_axis=1, concat_axis=1, tiled=True
        )
        return moved_back.reshape(slots, width)

    rows_all = send_rows(to_blocks(slot_input))
    preact = jnp.einsum("abjd,jdh->abjh", rows_all, up_weight, preferred_element_type=jnp.float32)
    active = gelu_tanh(preact).astype(jnp.bfloat16)
    partial_out = jnp.einsum(
        "abjh,jhd->abjd", active, down_weight, preferred_element_type=jnp.float32
    )
    preact, active, partial_out = (preact, active, partial_out)
    slot_output = return_rows(partial_out)
    grads_all = send_rows(to_blocks(slot_grad))
    grad_active = jnp.einsum(
        "abjd,jhd->abjh", grads_all, down_weight, preferred_element_type=jnp.float32
    )
    grad_pre = (grad_active * gelu_slope(preact)).astype(jnp.bfloat16)
    grad_second = jnp.einsum(
        "abjh,abjd->jhd", active, grads_all, preferred_element_type=jnp.float32
    ).astype(jnp.bfloat16)
    grad_first = jnp.einsum(
        "abjd,abjh->jdh", rows_all, grad_pre, preferred_element_type=jnp.float32
    ).astype(jnp.bfloat16)
    partial_in = jnp.einsum(
        "abjh,jdh->abjd", grad_pre, up_weight, preferred_element_type=jnp.float32
    )
    grad_first, grad_second, partial_in = (grad_first, grad_second, partial_in)
    slot_in_grad = return_rows(partial_in)
    grad_combine = lax.dot_general(
        image_grads, slot_output, over_cols, preferred_element_type=jnp.float32
    )
    combine_part = combine * (grad_combine - jnp.sum(combine * grad_combine, axis=1, keepdims=True))
    grad_dispatch = lax.dot_general(
        image_tokens, slot_in_grad, over_cols, preferred_element_type=jnp.float32
    )
    dispatch_part = dispatch * (
        grad_dispatch - jnp.sum(dispatch * grad_dispatch, axis=0, keepdims=True)
    )
    grad_logits = (combine_part + dispatch_part).astype(jnp.bfloat16)
    grad_image = jnp.dot(dispatch_b, slot_in_grad, preferred_element_type=jnp.float32)
    grad_image = grad_image + lax.dot_general(
        grad_logits, slot_param, over_cols, preferred_element_type=jnp.float32
    )
    param_term = lax.dot_general(
        image_tokens, grad_logits, over_rows, preferred_element_type=jnp.float32
    )
    param_grad = lax.psum(param_term, ("expert", "dp"))
    return (grad_image.astype(jnp.bfloat16)[None], param_grad, grad_first, grad_second)


def solution(mesh):
    return jax.shard_map(
        shards,
        mesh=mesh,
        in_specs=(
            P(("expert", "dp"), None, None),
            P(),
            P("expert", None, "dp"),
            P("expert", "dp", None),
            P(("expert", "dp"), None, None),
        ),
        out_specs=(
            P(("expert", "dp"), None, None),
            P(),
            P("expert", None, "dp"),
            P("expert", "dp", None),
        ),
        check_vma=False,
    )
```

profile of v0, /device:TPU:1, one launch (start us, length us, event | category | flops | bytes accessed | tf_op | source)
XLA Modules:
  0.0 428.0 jit_solution(2397438560726917814)
XLA Ops:
  7.2 1.9 fusion.69
  9.3 1.6 fusion.33
  11.7 2.0 reduce
  13.7 1.6 reshape.72
  15.3 13.5 %all-to-all-start.1 = ((bf16[64,2,512]{2,1,0:T(2,128)(2,1)}), bf16[64,2,512]{2,1,0:T(2,128)(2,1)S(1)}, u32[]{:S(2)}, u32[]{:S(2)}) async-start(bf16[64,2,512]{2,1,0:T(2,128)(2,1)} %reshape.72), calls=%async_computation.1 | async-start | bytes 262144 | tf_op jit(solution)/shard_map/all_to_all | solution.py:48
  29.3 1.4 reduce.1
  31.4 7.4 %all-to-all-done.1 = bf16[64,2,512]{2,1,0:T(2,128)(2,1)S(1)} async-done(((bf16[64,2,512]{2,1,0:T(2,128)(2,1)}), bf16[64,2,512]{2,1,0:T(2,128)(2,1)S(1)}, u32[]{:S(2)}, u32[]{:S(2)}) %all-to-all-start.1) | async-done | bytes 131104 | tf_op jit(solution)/shard_map/all_to_all | solution.py:48
  38.8 4.6 %all-to-all-start = ((bf16[64,2,512]{2,1,0:T(2,128)(2,1)}), bf16[64,2,512]{2,1,0:T(2,128)(2,1)S(1)}, u32[]{:S(2)}, u32[]{:S(2)}) async-start(bf16[64,2,512]{2,1,0:T(2,128)(2,1)} %reshape.74), calls=%async_computation | async-start | bytes 262144 | tf_op jit(solution)/shard_map/all_to_all | solution.py:48
  43.6 11.3 %all_gather.7 = bf16[4,64,1,1024]{3,1,2,0:T(8,128)(2,1)S(1)} all-gather(bf16[1,64,1,1024]{3,1,2,0:T(8,128)(2,1)S(1)} %copy.18), channel_id=1, replica_groups=mesh['expert'=64,'dp'=4] {'dp'}, dimensions={0}, use_global_device_ids=true | all-gather | bytes 655360 | tf_op jit(solution)/shard_map/all_gather | solution.py:49
  55.1 10.3 %all_gather.6 = bf16[4,64,1,1024]{3,1,2,0:T(8,128)(2,1)S(1)} all-gather(bf16[1,64,1,1024]{3,1,2,0:T(8,128)(2,1)S(1)} %copy.16), channel_id=1, replica_groups=mesh['expert'=64,'dp'=4] {'dp'}, dimensions={0}, use_global_device_ids=true | all-gather | bytes 655360 | tf_op jit(solution)/shard_map/all_gather | solution.py:49
  67.1 1.2 fusion.29
  68.3 1.7 fusion.20
  70.1 3.7 fusion.14
  73.9 3.6 fusion.9
  77.5 27.6 %reduce-scatter.3.cloned.1.call-done = f32[1,64,1,1024]{3,1,0,2:T(8,128)} async-done(((f32[4,64,1,1024]{3,1,0,2:T(8,128)}), f32[1,64,1,1024]{3,1,0,2:T(8,128)}) %reduce-scatter.3.cloned.1.call-update) | async-done | bytes 262160 | tf_op jit(solution)/shard_map/reduce_scatter | solution.py:52
  106.2 2.0 reduce.2
  108.2 1.6 reshape.76
  109.9 10.4 %all-to-all-start.2 = ((bf16[64,2,512]{2,1,0:T(2,128)(2,1)}), bf16[64,2,512]{2,1,0:T(2,128)(2,1)}, u32[]{:S(2)}, u32[]{:S(2)}) async-start(bf16[64,2,512]{2,1,0:T(2,128)(2,1)} %reshape.76), calls=%async_computation.3 | async-start | bytes 262144 | tf_op jit(solution)/shard_map/all_to_all | solution.py:53
  120.3 2.1 fusion.8
  122.4 22.1 %reduce-scatter.5.cloned.1.call-done = f32[1,64,1,1024]{3,1,0,2:T(8,128)} async-done(((f32[4,64,1,1024]{3,1,0,2:T(8,128)}), f32[1,64,1,1024]{3,1,0,2:T(8,128)}) %reduce-scatter.5.cloned.1.call-update) | async-done | bytes 262160 | tf_op jit(solution)/shard_map/reduce_scatter | solution.py:52
  145.6 2.1 reduce.3
  147.7 1.6 reshape.78
  149.4 10.4 %all-to-all-start.3 = ((bf16[64,2,512]{2,1,0:T(2,128)(2,1)}), bf16[64,2,512]{2,1,0:T(2,128)(2,1)}, u32[]{:S(2)}, u32[]{:S(2)}) async-start(bf16[64,2,512]{2,1,0:T(2,128)(2,1)} %reshape.78), calls=%async_computation.5 | async-start | bytes 262144 | tf_op jit(solution)/shard_map/all_to_all | solution.py:53
  159.9 1.4 reshape.77
  161.2 1.9 fusion.55
  163.1 1.1 convolution_bitcast_fusion.1
  164.2 5.4 %all-to-all-done.3 = bf16[64,2,512]{2,1,0:T(2,128)(2,1)} async-done(((bf16[64,2,512]{2,1,0:T(2,128)(2,1)}), bf16[64,2,512]{2,1,0:T(2,128)(2,1)}, u32[]{:S(2)}, u32[]{:S(2)}) %all-to-all-start.3) | async-done | bytes 131104 | tf_op jit(solution)/shard_map/all_to_all | solution.py:53
  169.6 2.0 reshape.79
  171.6 1.9 multiply_reduce_fusion.1
  175.3 3.2 fusion.10
  178.5 241.3 %all-reduce.2.cloned.1.call-done = f32[1024,64]{0,1:T(8,128)} async-done(((f32[1024,64]{0,1:T(8,128)}), f32[1024,64]{0,1:T(8,128)}) %all-reduce.2.cloned.1.call-update) | async-done | bytes 262160 | tf_op jit(solution)/shard_map/psum | solution.py:100
  419.8 1.7 copy.46
  (46 shorter events, 8.5 us)
Async XLA Ops:
  7.2 58.2 %copy-start = (bf16[1,1024,1024]{2,1,0:T(8,128)(2,1)S(1)}, bf16[1,1024,1024]{2,1,0:T(8,128)(2,1)}, u32[]{:S(2)}) copy-start(bf16[1,1024,1024]{2,1,0:T(8,128)(2,1)} %param.7) | copy-start | bytes 6291460
  7.2 21.6 %copy-start.2 = (bf16[1,512,1024]{2,1,0:T(8,128)(2,1)S(1)}, bf16[1,512,1024]{2,1,0:T(8,128)(2,1)}, u32[]{:S(2)}) copy-start(bf16[1,512,1024]{2,1,0:T(8,128)(2,1)} %param.9) | copy-start | bytes 3145732
  15.3 23.5 %all-to-all-start.1 = ((bf16[64,2,512]{2,1,0:T(2,128)(2,1)}), bf16[64,2,512]{2,1,0:T(2,128)(2,1)S(1)}, u32[]{:S(2)}, u32[]{:S(2)}) async-start(bf16[64,2,512]{2,1,0:T(2,128)(2,1)} %reshape.72), calls=%async_computation.1 | async-start | bytes 262144 | tf_op jit(solution)/shard_map/all_to_all | solution.py:48
  38.8 16.1 %all-to-all-start = ((bf16[64,2,512]{2,1,0:T(2,128)(2,1)}), bf16[64,2,512]{2,1,0:T(2,128)(2,1)S(1)}, u32[]{:S(2)}, u32[]{:S(2)}) async-start(bf16[64,2,512]{2,1,0:T(2,128)(2,1)} %reshape.74), calls=%async_computation | async-start | bytes 262144 | tf_op jit(solution)/shard_map/all_to_all | solution.py:48
  43.4 61.6 %reduce-scatter.3.cloned.1.call-start = ((), (), s32[]{:S(2)}) async-start(), calls=%async_computation.6 | async-start | bytes 1310720 | tf_op jit(solution)/shard_map/reduce_scatter | solution.py:52
  65.3 0.8 copy-start.5
  65.4 1.8 copy-start.9
  67.1 1.2 copy-start.10
  70.1 74.4 %reduce-scatter.5.cloned.1.call-start = ((), (), s32[]{:S(2)}) async-start(), calls=%async_computation.7 | async-start | bytes 1310720 | tf_op jit(solution)/shard_map/reduce_scatter | solution.py:52
  109.9 39.5 %all-to-all-start.2 = ((bf16[64,2,512]{2,1,0:T(2,128)(2,1)}), bf16[64,2,512]{2,1,0:T(2,128)(2,1)}, u32[]{:S(2)}, u32[]{:S(2)}) async-start(bf16[64,2,512]{2,1,0:T(2,128)(2,1)} %reshape.76), calls=%async_computation.3 | async-start | bytes 262144 | tf_op jit(solution)/shard_map/all_to_all | solution.py:53
  145.4 17.7 %copy-start.1 = (bf16[1,512,1024]{2,1,0:T(8,128)(2,1)S(1)}, bf16[1,512,1024]{2,1,0:T(8,128)(2,1)}, u32[]{:S(2)}) copy-start(bf16[1,512,1024]{2,1,0:T(8,128)(2,1)} %param.5) | copy-start | bytes 3145732
  149.4 20.3 %all-to-all-start.3 = ((bf16[64,2,512]{2,1,0:T(2,128)(2,1)}), bf16[64,2,512]{2,1,0:T(2,128)(2,1)}, u32[]{:S(2)}, u32[]{:S(2)}) async-start(bf16[64,2,512]{2,1,0:T(2,128)(2,1)} %reshape.78), calls=%async_computation.5 | async-start | bytes 262144 | tf_op jit(solution)/shard_map/all_to_all | solution.py:53
  159.8 259.9 %all-reduce.2.cloned.1.call-start = ((), (), s32[]{:S(2)}) async-start(), calls=%async_computation.8 | async-start | bytes 524288 | tf_op jit(solution)/shard_map/psum | solution.py:100
  164.2 9.9 %copy-start.4 = (f32[512,64]{0,1:T(8,128)S(1)}, f32[512,64]{0,1:T(8,128)}, u32[]{:S(2)}) copy-start(f32[512,64]{0,1:T(8,128)} %convolution_bitcast_fusion.1) | copy-start | bytes 393220
  171.6 3.7 copy-start.3
  173.5 0.7 copy-start.6
  173.5 0.6 copy-start.7
  173.5 0.6 copy-start.8
Sparse Core Ops, SparseCore 0:
  70.2 34.7 reduce-scatter.2
  108.0 36.3 reduce-scatter.4
  175.4 244.3 all-reduce.1
where the time goes:
time: 429 us; the launch traced here: 428 us
  waiting for transfers between devices  304 us (71%)
  starting transfers between devices  39.1 us (9%)
  matrix products  26 us (6%)
  blocking collectives  21.6 us (5%)
  local copies, waits for them, and re-layouts  14 us (3%)
  between operations  14 us (3%)
  other arithmetic  9.59 us (2%)
    psum x1, waiting for transfers between devices, shards(): param_grad = lax.psum(param_term, ('expert', 'dp'))  241 us
    reduce_scatter x2, waiting for transfers between devices, return_rows(): lax.psum_scatter(partial_rows, 'dp', scatter_dimension=0, tiled=True)  49.6 us
    all_gather x2, blocking collectives, send_rows(): return lax.all_gather(moved_rows, 'dp', axis=0, tiled=True)  21.6 us
    all_to_all x2, starting transfers between devices, return_rows(): lax.all_to_all(summed_rows.astype(jnp.bfloat16), 'expert', split_axis=1,...  20.9 us
    all_to_all x2, starting transfers between devices, send_rows(): lax.all_to_all(blocks, 'expert', split_axis=1, concat_axis=1, tiled=True)  18.1 us
    unnamed x32, local copies, waits for them, and re-layouts  13.1 us
  transfers between devices with their start and end apart: 7, of which 5 were waited for; matrix products, arithmetic and copies ran while one was open for 7% of the time, Pallas kernels for 0%

commit v1 on v0

v1 whole, which is shorter than its diff:
```python
import jax
import jax.numpy as jnp
from jax import lax
from jax.sharding import Mesh, PartitionSpec as P

gelu_coeff = 0.7978845608
cubic_coeff = 0.044715

CHIPS = ("x", "y_lo", "z", "y_hi")
EXPERT = ("x", "y_lo", "z")
DP = ("y_hi", "core")


def gelu_tanh(values):
    inner = gelu_coeff * (values + cubic_coeff * values * values * values)
    return 0.5 * values * (1.0 + jnp.tanh(inner))


def gelu_slope(values):
    inner = gelu_coeff * (values + cubic_coeff * values * values * values)
    tangent = jnp.tanh(inner)
    return 0.5 * (1.0 + tangent) + 0.5 * values * (1.0 - tangent * tangent) * gelu_coeff * (
        1.0 + 3.0 * cubic_coeff * values * values
    )


def dot(a, b, dims):
    return lax.dot_general(a, b, (dims, ((), ())), preferred_element_type=jnp.float32)


def swap_cores(values):
    return lax.ppermute(values, "core", [(0, 1), (1, 0)])


def exchange(blocks):
    return lax.all_to_all(blocks, CHIPS, 0, 0, tiled=True)


def shards(tokens, slot_param, up_weight, down_weight, grad_output):
    image_tokens = tokens[0]
    image_grads = grad_output[0]
    up = up_weight[0]
    down = down_weight[0]
    bf16 = jnp.bfloat16
    chips = lax.axis_size(CHIPS)
    slots = slot_param.shape[1]
    width = tokens.shape[2]
    core = lax.axis_index("core")
    param_t = slot_param.T
    logits = dot(param_t, image_tokens, ((1,), (1,)))
    dispatch = jax.nn.softmax(logits, axis=1)
    combine = jax.nn.softmax(logits, axis=0)
    dispatch_b = dispatch.astype(bf16)
    slot_input = dot(dispatch_b, image_tokens, ((1,), (0,))).astype(bf16)
    slot_grad = dot(combine.astype(bf16), image_grads, ((1,), (0,))).astype(bf16)
    rows = jnp.concatenate(
        [slot_input.reshape(slots, 1, 8, 128), slot_grad.reshape(slots, 1, 8, 128)], axis=2
    )
    copies = lax.axis_size("y_hi")
    rows = jnp.broadcast_to(rows, (slots, copies, 16, 128)).reshape(chips, 16, 128)
    mine = exchange(rows)
    both = jnp.concatenate([mine, swap_cores(mine)], axis=0).reshape(2 * chips, 2, width)
    rows_in = both[:, 0]
    rows_grad = both[:, 1]
    preact = dot(rows_in, up, ((1,), (0,)))
    active = gelu_tanh(preact).astype(bf16)
    partial_out = dot(active, down, ((1,), (0,))).astype(bf16)
    grad_active = dot(rows_grad, down, ((1,), (1,)))
    grad_pre = (grad_active * gelu_slope(preact)).astype(bf16)
    partial_in = dot(grad_pre, up, ((1,), (1,))).astype(bf16)
    grad_down = dot(active, rows_grad, ((0,), (0,))).astype(bf16)
    grad_up = dot(rows_in, grad_pre, ((0,), (0,))).astype(bf16)
    partial = jnp.stack([partial_out, partial_in], axis=1).reshape(2, chips, 16, 128)
    summed = partial[0].astype(jnp.float32) + swap_cores(partial[1]).astype(jnp.float32)
    returned = exchange(summed.astype(bf16)).reshape(slots, copies, 2, width)
    returned = jnp.sum(returned.astype(jnp.float32), axis=1).astype(bf16)
    slot_output = returned[:, 0]
    slot_in_grad = returned[:, 1]
    grad_combine = dot(slot_output, image_grads, ((1,), (1,)))
    combine_part = combine * (grad_combine - jnp.sum(combine * grad_combine, axis=0, keepdims=True))
    grad_dispatch = dot(slot_in_grad, image_tokens, ((1,), (1,)))
    dispatch_part = dispatch * (
        grad_dispatch - jnp.sum(dispatch * grad_dispatch, axis=1, keepdims=True)
    )
    grad_logits = (combine_part + dispatch_part).astype(bf16)
    left = jnp.concatenate([dispatch_b, grad_logits], axis=0)
    right = jnp.concatenate([slot_in_grad, param_t], axis=0)
    grad_image = dot(left, right, ((0,), (0,)))
    param_term = dot(grad_logits, image_tokens, ((1,), (0,)))
    halves = param_term.reshape(2, slots // 2, width)
    kept = lax.dynamic_index_in_dim(halves, core, 0, keepdims=False)
    sent = lax.dynamic_index_in_dim(halves, 1 - core, 0, keepdims=False)
    kept = kept + swap_cores(sent)
    blocks = kept.reshape(chips, -1, 128)
    block = jnp.sum(exchange(blocks), axis=0, keepdims=True)
    half = exchange(jnp.broadcast_to(block, blocks.shape)).reshape(1, slots // 2, width)
    other = swap_cores(half)
    first = jnp.where(core == 0, half, other)
    second = jnp.where(core == 0, other, half)
    param_grad = jnp.concatenate([first, second], axis=0).reshape(slots, width).T
    return (grad_image.astype(bf16)[None], param_grad, grad_up[None], grad_down[None])


def solution(mesh):
    devices = mesh.devices.reshape(4, 2, 8, 2, 2)
    cut = Mesh(devices, ("x", "y_lo", "z", "y_hi", "core"))
    return jax.shard_map(
        shards,
        mesh=cut,
        in_specs=(
            P(EXPERT + DP, None, None),
            P(),
            P(EXPERT, None, DP),
            P(EXPERT, DP, None),
            P(EXPERT + DP, None, None),
        ),
        out_specs=(
            P(EXPERT + DP, None, None),
            P(),
            P(EXPERT, None, DP),
            P(EXPERT, DP, None),
        ),
        check_vma=False,
    )
```

time: 429 us -> 144 us (0.34)
  waiting for transfers between devices: 304 us -> 26.1 us
  blocking collectives: 21.6 us -> 50.4 us
  starting transfers between devices: 39.1 us -> 25.2 us
  between operations: 14 us -> 0.95 us
  matrix products: 26 us -> 19.6 us
    psum x1 -> x0, waiting for transfers between devices: 241 us -> none  [shards(): param_grad = lax.psum(param_term, ('expert', 'dp'))]
    all_to_all x0 -> x2, blocking collectives: none -> 50.4 us  [exchange(): return lax.all_to_all(blocks, CHIPS, 0, 0, tiled=True)]
    reduce_scatter x2 -> x0, waiting for transfers between devices: 49.6 us -> none  [return_rows(): lax.psum_scatter(partial_rows, 'dp', scatter_dimension=0, tiled=True)]
    all_to_all x4 -> x2, starting transfers between devices: 39 us -> 15 us  [exchange(): return lax.all_to_all(blocks, CHIPS, 0, 0, tiled=True)]
    all_gather x2 -> x0, blocking collectives: 21.6 us -> none  [send_rows(): return lax.all_gather(moved_rows, 'dp', axis=0, tiled=True)]
    unnamed x32 -> x29, local copies, waits for them, and re-layouts: 13.1 us -> 2.09 us
    ppermute x0 -> x4, starting transfers between devices: none -> 10.2 us  [swap_cores(): return lax.ppermute(values, 'core', [(0, 1), (1, 0)])]
    all_to_all x4 -> x2, waiting for transfers between devices: 12.8 us -> 23 us  [exchange(): return lax.all_to_all(blocks, CHIPS, 0, 0, tiled=True)]
  transfers between devices with their start and end apart: 7 -> 6, of which waited for: 5 -> 5; matrix products, arithmetic and copies ran while one was open for 7% -> 7% of each run, Pallas kernels for 0% -> 0%
where the time goes in v1:
time: 144 us; the launch traced here: 143 us
  blocking collectives  50.4 us (35%)
  waiting for transfers between devices  26.1 us (18%)
  starting transfers between devices  25.2 us (18%)
  matrix products  19.6 us (14%)
  local copies, waits for them, and re-layouts  13.1 us (9%)
  other arithmetic  7.68 us (5%)
    all_to_all x2, blocking collectives, exchange(): return lax.all_to_all(blocks, CHIPS, 0, 0, tiled=True)  50.4 us
    all_to_all x2, waiting for transfers between devices, exchange(): return lax.all_to_all(blocks, CHIPS, 0, 0, tiled=True)  23 us
    dot_general x13, matrix products, dot(): lax.dot_general(a, b, (dims, ((), ())), preferred_element_type=jnp.float32)  19.6 us
    all_to_all x2, starting transfers between devices, exchange(): return lax.all_to_all(blocks, CHIPS, 0, 0, tiled=True)  15 us
    ppermute x4, starting transfers between devices, swap_cores(): return lax.ppermute(values, 'core', [(0, 1), (1, 0)])  10.2 us
    ppermute x4, waiting for transfers between devices, swap_cores(): return lax.ppermute(values, 'core', [(0, 1), (1, 0)])  3.11 us
  transfers between devices with their start and end apart: 6, of which 5 were waited for; matrix products, arithmetic and copies ran while one was open for 7% of the time, Pallas kernels for 0%

profile of v1, /device:TPU:1, one launch (start us, length us, event | category | flops | bytes accessed | tf_op | source)
XLA Modules:
  0.0 143.2 jit_solution(7964529980080582630)
XLA Ops:
  0.7 2.0 %fusion.62 = (f32[64]{0:T(128)S(1)}, f32[512]{0:T(512)S(1)}, f32[64,512]{1,0:T(8,128)S(1)}) fusion(bf16[1024,64]{0,1:T(8,128)(2,1)} %param.6, bf16[1,512,1024]{2,1,0:T(8,128)(2,1)} %param.5), kind=kOutput, calls=%fused_computation.76 | convolution fusion | flops 67173824 | bytes 1313024 | tf_op jit(solution)/shard_map/dot_general | solution.py:28
  3.0 1.6 %fusion.27 = bf16[8,8,8,128]{3,1,2,0:T(8,128)(2,1)S(1)} fusion(bf16[64,512]{1,0:T(8,128)(2,1)S(1)} %fusion.61, bf16[1,512,1024]{2,1,0:T(8,128)(2,1)} %param.5), kind=kOutput, calls=%fused_computation.22 | convolution fusion | flops 67174400 | bytes 1245184 | tf_op jit(solution)/shard_map/dot_general | solution.py:28
  5.1 32.6 %all_to_all.20 = bf16[128,16,128]{2,1,0:T(8,128)(2,1)S(1)} all-to-all(bf16[128,16,128]{2,1,0:T(8,128)(2,1)S(1)} %bitcast.107), channel_id=1, replica_groups=mesh['x'=4,'y_lo'=2,'z'=8,'y_hi'=2,'core'=2] {'x','y_lo','z','y_hi'}, dimensions={0} | all-to-all | bytes 1048576 | tf_op jit(solution)/shard_map/all_to_all | solution.py:36
  37.7 3.7 %collective-permute-start = (bf16[128,16,128]{2,1,0:T(8,128)(2,1)S(1)}, bf16[128,16,128]{2,1,0:T(8,128)(2,1)S(1)}, u32[]{:S(2)}, u32[]{:S(2)}) collective-permute-start(bf16[128,16,128]{2,1,0:T(8,128)(2,1)S(1)} %all_to_all.20), channel_id=1, source_target_pairs={{0,1},{1,0},{2,3},{3,2},{4,5},{5,4},{6,7},{7,6},{8,9},{9,8},{10,11... | collective-permute-start | bytes 1572872 | tf_op jit(solution)/shard_map/ppermute | solution.py:32
  41.4 1.5 %collective-permute-done = bf16[128,16,128]{2,1,0:T(8,128)(2,1)S(1)} collective-permute-done((bf16[128,16,128]{2,1,0:T(8,128)(2,1)S(1)}, bf16[128,16,128]{2,1,0:T(8,128)(2,1)S(1)}, u32[]{:S(2)}, u32[]{:S(2)}) %collective-permute-start) | collective-permute-done | bytes 524320 | tf_op jit(solution)/shard_map/ppermute | solution.py:32
  43.0 1.1 pad_maximum_fusion
  44.0 1.6 %copy.29 = bf16[256,16,128]{0,2,1:T(8,128)(2,1)S(1)} copy(bf16[256,16,128]{2,1,0:T(8,128)(2,1)} %pad_maximum_fusion) | data formatting | bytes 2097152 | tf_op jit(solution)/shard_map/concatenate | solution.py:62
  45.7 2.7 %fusion.6 = f32[256,1024]{1,0:T(8,128)S(1)} fusion(bf16[1,1024,1024]{2,1,0:T(8,128)(2,1)} %param.7, bf16[256,2,1024]{0,2,1:T(8,128)(2,1)S(1)} %bitcast.102), kind=kOutput, calls=%fused_computation.6 | convolution fusion | flops 536870912 | bytes 3670016 | tf_op jit(solution)/shard_map/dot_general | solution.py:28
  48.4 1.3 fusion.18
  49.7 0.8 fusion.21
  50.6 0.9 copy-done.4
  51.5 0.7 fusion.24
  52.2 0.9 pad_maximum_fusion.1
  53.2 2.0 %copy.33 = bf16[128,2,1024]{0,2,1:T(8,128)(2,1)} copy(bf16[128,2,1024]{2,0,1:T(8,128)(2,1)} %get-tuple-element.10) | data formatting | bytes 1048576 | tf_op jit(solution)/shard_map/slice | solution.py:74
  55.6 1.3 copy.32
  57.5 1.5 %add_convert_fusion = bf16[128,16,128]{0,2,1:T(8,128)(2,1)S(1)} fusion(f32[128,16,128]{0,2,1:T(8,128)} %bitcast.106, bf16[128,16,128]{0,2,1:T(8,128)(2,1)} %collective-permute-done.1), kind=kLoop, calls=%fused_computation.42 | loop fusion | flops 786432 | bytes 2097152 | tf_op jit(solution)/shard_map/convert_element_type | solution.py:75
  59.0 1.2 copy.34
  60.2 7.7 %all-to-all-start.1 = ((bf16[128,16,128]{2,1,0:T(8,128)(2,1)}), bf16[128,16,128]{2,1,0:T(8,128)(2,1)}, u32[]{:S(2)}, u32[]{:S(2)}) async-start(bf16[128,16,128]{2,1,0:T(8,128)(2,1)} %copy.34), calls=%async_computation.1 | async-start | bytes 1048576 | tf_op jit(solution)/shard_map/all_to_all | solution.py:36
  67.9 16.3 %all-to-all-done.1 = bf16[128,16,128]{2,1,0:T(8,128)(2,1)} async-done(((bf16[128,16,128]{2,1,0:T(8,128)(2,1)}), bf16[128,16,128]{2,1,0:T(8,128)(2,1)}, u32[]{:S(2)}, u32[]{:S(2)}) %all-to-all-start.1) | async-done | bytes 524320 | tf_op jit(solution)/shard_map/all_to_all | solution.py:36
  84.2 2.0 %reshape.52 = bf16[64,2,2,1024]{3,2,1,0:T(2,128)(2,1)} reshape(bf16[128,16,128]{2,1,0:T(8,128)(2,1)} %all-to-all-done.1) | data formatting | bytes 1048576 | tf_op jit(solution)/shard_map/reshape | solution.py:75
  86.1 1.9 %reduce_sum.59 = bf16[64,2,1024]{2,1,0:T(2,128)(2,1)S(1)} reduce(bf16[64,2,2,1024]{3,2,1,0:T(2,128)(2,1)} %reshape.52, bf16[]{:T(256)} %constant.12.clone.1), dimensions={1}, to_apply=%region_4.0 | reduce | flops 131072 | bytes 786434 | tf_op jit(solution)/shard_map/reduce_sum | solution.py:76
  90.9 3.3 %collective-permute-start.2 = (f32[32,1024]{1,0:T(8,128)S(1)}, f32[32,1024]{1,0:T(8,128)S(1)}, u32[]{:S(2)}, u32[]{:S(2)}) collective-permute-start(f32[32,1024]{1,0:T(8,128)S(1)} %dynamic-slice_bitcast_fusion), channel_id=1, source_target_pairs={{0,1},{1,0},{2,3},{3,2},{4,5},{5,4},{6,7},{7,6},{8,9},{9,8},{10,11... | collective-permute-start | bytes 393224 | tf_op jit(solution)/shard_map/ppermute | solution.py:32
  94.1 1.0 collective-permute-done.2
  95.1 0.9 bitcast_add_fusion
  96.2 17.8 %all_to_all.21 = f32[128,2,128]{2,1,0:T(2,128)S(1)} all-to-all(f32[128,2,128]{2,1,0:T(2,128)S(1)} %reshape.53), channel_id=1, replica_groups=mesh['x'=4,'y_lo'=2,'z'=8,'y_hi'=2,'core'=2] {'x','y_lo','z','y_hi'}, dimensions={0} | all-to-all | bytes 262144 | tf_op jit(solution)/shard_map/all_to_all | solution.py:36
  114.8 7.3 %all-to-all-start.3 = ((f32[128,2,128]{2,1,0:T(2,128)}), f32[128,2,128]{2,1,0:T(2,128)}, u32[]{:S(2)}, u32[]{:S(2)}) async-start(f32[128,2,128]{2,1,0:T(2,128)} %broadcast_in_dim.15), calls=%async_computation.3 | async-start | bytes 262144 | tf_op jit(solution)/shard_map/all_to_all | solution.py:36
  122.1 3.7 %convert_bitcast_fusion = bf16[1,1024,1024]{2,1,0:T(8,128)(2,1)} fusion(bf16[256,2,1024]{0,2,1:T(8,128)(2,1)} %bitcast.104, f32[256,1024]{1,0:T(8,128)} %copy-done.5), kind=kOutput, calls=%fused_computation.8 | convolution fusion | flops 540278784 | bytes 3670016 | tf_op jit(solution)/shard_map/dot_general | solution.py:28
  125.8 6.7 %all-to-all-done.3 = f32[128,2,128]{2,1,0:T(2,128)} async-done(((f32[128,2,128]{2,1,0:T(2,128)}), f32[128,2,128]{2,1,0:T(2,128)}, u32[]{:S(2)}, u32[]{:S(2)}) %all-to-all-start.3) | async-done | bytes 131104 | tf_op jit(solution)/shard_map/all_to_all | solution.py:36
  132.5 1.7 %reshape.54 = f32[1,32,1024]{2,1,0:T(8,128)} reshape(f32[128,2,128]{2,1,0:T(2,128)} %all-to-all-done.3) | data formatting | bytes 262144 | tf_op jit(solution)/shard_map/reshape | solution.py:96
  134.1 2.9 %collective-permute-start.3 = (f32[1,32,1024]{2,1,0:T(8,128)}, f32[1,32,1024]{2,1,0:T(8,128)S(1)}, u32[]{:S(2)}, u32[]{:S(2)}) collective-permute-start(f32[1,32,1024]{2,1,0:T(8,128)} %reshape.54), channel_id=1, source_target_pairs={{0,1},{1,0},{2,3},{3,2},{4,5},{5,4},{6,7},{7,6},{8,9},{9,8},{10,11... | collective-permute-start | bytes 393224 | tf_op jit(solution)/shard_map/ppermute | solution.py:32
  137.0 3.1 %convert_bitcast_fusion.1 = bf16[1,1024,1024]{2,1,0:T(8,128)(2,1)} fusion(bf16[256,1024]{1,0:T(8,128)(2,1)} %copy-done.12, bf16[256,2,1024]{0,2,1:T(8,128)(2,1)S(1)} %bitcast.105), kind=kOutput, calls=%fused_computation.9 | convolution fusion | flops 537919488 | bytes 3145728 | tf_op jit(solution)/shard_map/dot_general | solution.py:28
  140.1 2.3 %fusion.8 = bf16[1,512,1024]{2,1,0:T(8,128)(2,1)} fusion(bf16[64,1024]{1,0:T(8,128)(2,1)} %bitcast.114, bf16[64,1024]{1,0:T(8,128)(2,1)S(1)} %bitcast.109, bf16[64,512]{1,0:T(8,128)(2,1)S(1)} %add_convert_fusion.1, bf16[64,512]{1,0:T(8,128)(2,1)S(1)} %copy-done.10), kind=kOutput, calls=%fused_computation.13 | convolution fusion | flops 135528448 | bytes 1441792 | tf_op jit(solution)/shard_map/dot_general | solution.py:28
  (47 shorter events, 6.2 us)
Async XLA Ops:
  0.6 47.8 %copy-start = (bf16[1,1024,1024]{2,1,0:T(8,128)(2,1)S(1)}, bf16[1,1024,1024]{2,1,0:T(8,128)(2,1)}, u32[]{:S(2)}) copy-start(bf16[1,1024,1024]{2,1,0:T(8,128)(2,1)} %param.8) | copy-start | bytes 6291460
  0.6 3.9 %copy-start.6 = (bf16[1,512,1024]{2,1,0:T(8,128)(2,1)S(1)}, bf16[1,512,1024]{2,1,0:T(8,128)(2,1)}, u32[]{:S(2)}) copy-start(bf16[1,512,1024]{2,1,0:T(8,128)(2,1)} %param.9) | copy-start | bytes 3145732
  3.0 1.9 %copy-start.9 = (bf16[64,512]{1,0:T(8,128)(2,1)}, bf16[64,512]{1,0:T(8,128)(2,1)S(1)}, u32[]{:S(2)}) copy-start(bf16[64,512]{1,0:T(8,128)(2,1)S(1)} %fusion.61) | copy-start | bytes 196612
  37.7 5.3 %collective-permute-start = (bf16[128,16,128]{2,1,0:T(8,128)(2,1)S(1)}, bf16[128,16,128]{2,1,0:T(8,128)(2,1)S(1)}, u32[]{:S(2)}, u32[]{:S(2)}) collective-permute-start(bf16[128,16,128]{2,1,0:T(8,128)(2,1)S(1)} %all_to_all.20), channel_id=1, source_target_pairs={{0,1},{1,0},{2,3},{3,2},{4,5},{5,4},{6,7},{7,6},{8,9},{9,8},{10,11... | collective-permute-start | bytes 1572872 | tf_op jit(solution)/shard_map/ppermute | solution.py:32
  45.7 4.0 %copy-start.2 = (bf16[256,16,128]{0,2,1:T(8,128)(2,1)}, bf16[256,16,128]{0,2,1:T(8,128)(2,1)S(1)}, u32[]{:S(2)}) copy-start(bf16[256,16,128]{0,2,1:T(8,128)(2,1)S(1)} %copy.29) | copy-start | bytes 3145732
  48.4 1.3 copy-start.5
  49.7 0.9 copy-start.12
  49.7 1.8 %copy-start.4 = (bf16[1,1024,1024]{2,1,0:T(8,128)(2,1)S(1)}, bf16[1,1024,1024]{2,1,0:T(8,128)(2,1)}, u32[]{:S(2)}) copy-start(bf16[1,1024,1024]{2,1,0:T(8,128)(2,1)} %param.7) | copy-start | bytes 6291460
  55.2 2.3 %collective-permute-start.1 = (bf16[128,16,128]{0,2,1:T(8,128)(2,1)}, bf16[128,16,128]{0,2,1:T(8,128)(2,1)}, u32[]{:S(2)}, u32[]{:S(2)}) collective-permute-start(bf16[128,16,128]{0,2,1:T(8,128)(2,1)} %bitcast.111), channel_id=1, source_target_pairs={{0,1},{1,0},{2,3},{3,2},{4,5},{5,4},{6,7},{7,6},{8,9},{9,8},{10,11... | collective-permute-start | bytes 1572872 | tf_op jit(solution)/shard_map/ppermute | solution.py:32
  60.2 28.3 %copy-start.1 = (bf16[1,512,1024]{2,1,0:T(8,128)(2,1)S(1)}, bf16[1,512,1024]{2,1,0:T(8,128)(2,1)}, u32[]{:S(2)}) copy-start(bf16[1,512,1024]{2,1,0:T(8,128)(2,1)} %param.5) | copy-start | bytes 3145732
  60.2 24.0 %all-to-all-start.1 = ((bf16[128,16,128]{2,1,0:T(8,128)(2,1)}), bf16[128,16,128]{2,1,0:T(8,128)(2,1)}, u32[]{:S(2)}, u32[]{:S(2)}) async-start(bf16[128,16,128]{2,1,0:T(8,128)(2,1)} %copy.34), calls=%async_computation.1 | async-start | bytes 1048576 | tf_op jit(solution)/shard_map/all_to_all | solution.py:36
  88.0 1.2 copy-start.7
  90.1 0.7 copy-start.8
  90.9 4.3 %collective-permute-start.2 = (f32[32,1024]{1,0:T(8,128)S(1)}, f32[32,1024]{1,0:T(8,128)S(1)}, u32[]{:S(2)}, u32[]{:S(2)}) collective-permute-start(f32[32,1024]{1,0:T(8,128)S(1)} %dynamic-slice_bitcast_fusion), channel_id=1, source_target_pairs={{0,1},{1,0},{2,3},{3,2},{4,5},{5,4},{6,7},{7,6},{8,9},{9,8},{10,11... | collective-permute-start | bytes 393224 | tf_op jit(solution)/shard_map/ppermute | solution.py:32
  114.8 17.7 %all-to-all-start.3 = ((f32[128,2,128]{2,1,0:T(2,128)}), f32[128,2,128]{2,1,0:T(2,128)}, u32[]{:S(2)}, u32[]{:S(2)}) async-start(f32[128,2,128]{2,1,0:T(2,128)} %broadcast_in_dim.15), calls=%async_computation.3 | async-start | bytes 262144 | tf_op jit(solution)/shard_map/all_to_all | solution.py:36
  122.1 14.9 %copy-start.3 = (bf16[256,16,128]{0,2,1:T(8,128)(2,1)S(1)}, bf16[256,16,128]{0,2,1:T(8,128)(2,1)}, u32[]{:S(2)}) copy-start(bf16[256,16,128]{0,2,1:T(8,128)(2,1)} %copy-done.2) | copy-start | bytes 3145732
  125.8 14.3 %copy-start.10 = (bf16[64,512]{1,0:T(8,128)(2,1)S(1)}, bf16[64,512]{1,0:T(8,128)(2,1)}, u32[]{:S(2)}) copy-start(bf16[64,512]{1,0:T(8,128)(2,1)} %copy-done.9) | copy-start | bytes 196612
  134.1 8.3 %copy-start.11 = (f32[1,32,1024]{2,1,0:T(8,128)S(1)}, f32[1,32,1024]{2,1,0:T(8,128)}, u32[]{:S(2)}) copy-start(f32[1,32,1024]{2,1,0:T(8,128)} %reshape.54) | copy-start | bytes 393220
  134.1 8.3 %collective-permute-start.3 = (f32[1,32,1024]{2,1,0:T(8,128)}, f32[1,32,1024]{2,1,0:T(8,128)S(1)}, u32[]{:S(2)}, u32[]{:S(2)}) collective-permute-start(f32[1,32,1024]{2,1,0:T(8,128)} %reshape.54), channel_id=1, source_target_pairs={{0,1},{1,0},{2,3},{3,2},{4,5},{5,4},{6,7},{7,6},{8,9},{9,8},{10,11... | collective-permute-start | bytes 393224 | tf_op jit(solution)/shard_map/ppermute | solution.py:32

commit v2 on v1

v2 whole, which is shorter than its diff:
```python
import functools

import jax
import jax.numpy as jnp
from jax import lax
from jax.experimental import pallas as pl
from jax.experimental.pallas import tpu as pltpu
from jax.sharding import Mesh, PartitionSpec as P

gelu_coeff = 0.7978845608
cubic_coeff = 0.044715

CHIPS = ("x", "y_lo", "z", "y_hi")
EXPERT = ("x", "y_lo", "z")
DP = ("y_hi", "core")
F32 = jnp.float32
BF16 = jnp.bfloat16
LANES = 128


def dot(a, b, dims):
    return lax.dot_general(a, b, (dims, ((), ())), preferred_element_type=F32)


def swap_cores(values):
    return lax.ppermute(values, "core", [(0, 1), (1, 0)])


def exchange(blocks):
    return lax.all_to_all(blocks, CHIPS, 0, 0, tiled=True)


def call(kernel, outs, scratch=(), flops=0, moved=0, scalars=0, limit=24):
    def run(*args):
        specs = [
            pl.BlockSpec(memory_space=pltpu.SMEM if i < scalars else pltpu.VMEM)
            for i in range(len(args))
        ]
        return pl.pallas_call(
            kernel,
            out_shape=[jax.ShapeDtypeStruct(shape, dtype) for shape, dtype in outs],
            in_specs=specs,
            out_specs=[pl.BlockSpec(memory_space=pltpu.VMEM) for _ in outs],
            scratch_shapes=[pltpu.VMEM(shape, dtype) for shape, dtype in scratch],
            compiler_params=pltpu.CompilerParams(vmem_limit_bytes=limit << 20),
            cost_estimate=pl.CostEstimate(flops=flops, bytes_accessed=moved, transcendentals=0),
        )(*args)

    return run


def to_blocks(scratch, values, first, rows, start=0):
    for k in range(values.shape[1] // LANES):
        scratch[pl.ds(start + first + k, rows, stride=16), :] = values[:, k * LANES : (k + 1) * LANES]


def front_kernel(tokens, grads, param, rows, dispatch, combine, lines):
    slots = param.shape[0]
    logits = dot(param[...], tokens[...], ((1,), (1,)))
    e = jnp.exp(logits - jnp.max(logits, axis=1, keepdims=True))
    d = e / jnp.sum(e, axis=1, keepdims=True)
    e = jnp.exp(logits - jnp.max(logits, axis=0, keepdims=True))
    c = e / jnp.sum(e, axis=0, keepdims=True)
    dispatch[...] = d
    combine[...] = c
    to_blocks(lines, dot(d.astype(BF16), tokens[...], ((1,), (0,))), 0, slots)
    to_blocks(lines, dot(c.astype(BF16), grads[...], ((1,), (0,))), 8, slots)
    blocks = lines[...].reshape(slots, 16, LANES).astype(BF16)
    for copy in range(rows.shape[1]):
        rows[:, copy] = blocks


def expert_kernel(mine, theirs, up, down, own, send, active, grad_pre, rows_in, rows_grad, lines):
    images = mine.shape[0]
    count = 2 * images
    width = up.shape[0]
    hidden = up.shape[1]
    lines[: images * 16, :] = mine[...].reshape(images * 16, LANES).astype(F32)
    lines[images * 16 :, :] = theirs[...].reshape(images * 16, LANES).astype(F32)
    for k in range(8):
        cols = slice(k * LANES, (k + 1) * LANES)
        rows_in[:, cols] = lines[pl.ds(k, count, stride=16), :].astype(BF16)
        rows_grad[:, cols] = lines[pl.ds(8 + k, count, stride=16), :].astype(BF16)
    for c in range(0, hidden, 256):
        cols = slice(c, c + 256)
        v = dot(rows_in[...], up[:, cols], ((1,), (0,)))
        tangent = jnp.tanh(gelu_coeff * (v + cubic_coeff * v * v * v))
        active[:, cols] = (0.5 * v * (1.0 + tangent)).astype(BF16)
        slope = 0.5 * (1.0 + tangent) + 0.5 * v * (1.0 - tangent * tangent) * gelu_coeff * (
            1.0 + 3.0 * cubic_coeff * v * v
        )
        g = dot(rows_grad[...], down[cols, :], ((1,), (1,)))
        grad_pre[:, cols] = (g * slope).astype(BF16)
    for n in range(0, width, 256):
        cols = slice(n, n + 256)
        to_blocks(lines, dot(active[...], down[:, cols], ((1,), (0,))), n // LANES, count)
        to_blocks(lines, dot(grad_pre[...], up[cols, :], ((1,), (1,))), 8 + n // LANES, count)
    own[...] = lines[: images * 16, :].reshape(images, 16, LANES)
    send[...] = lines[images * 16 :, :].reshape(images, 16, LANES).astype(BF16)


def weights_kernel(rows_in, grad_pre, active, rows_grad, grad_up, grad_down):
    grad_up[...] = dot(rows_in[...], grad_pre[...], ((0,), (0,))).astype(BF16)
    grad_down[...] = dot(active[...], rows_grad[...], ((0,), (0,))).astype(BF16)


def weight_grads(rows_in, grad_pre, active, rows_grad):
    count, width = rows_in.shape
    hidden = active.shape[1]
    step = 256
    part = pl.BlockSpec((count, step), lambda i: (0, i))
    whole = lambda n: pl.BlockSpec((count, n), lambda i: (0, 0))
    return pl.pallas_call(
        weights_kernel,
        grid=(width // step,),
        out_shape=[
            jax.ShapeDtypeStruct((width, hidden), BF16),
            jax.ShapeDtypeStruct((hidden, width), BF16),
        ],
        in_specs=[part, whole(hidden), part, whole(width)],
        out_specs=[
            pl.BlockSpec((step, hidden), lambda i: (i, 0)),
            pl.BlockSpec((step, width), lambda i: (i, 0)),
        ],
        compiler_params=pltpu.CompilerParams(vmem_limit_bytes=16 << 20),
        cost_estimate=pl.CostEstimate(
            flops=4 * count * width * hidden, bytes_accessed=4 * width * hidden, transcendentals=0
        ),
    )(rows_in, grad_pre, active, rows_grad)


def back_kernel(core, returned, tokens, grads, dispatch, combine, logit_grads, slot_grads, kept, sent, lines, halves):
    slots = logit_grads.shape[0]
    width = tokens.shape[1]
    total = returned[:, 0].astype(F32)
    for copy in range(1, returned.shape[1]):
        total = total + returned[:, copy].astype(F32)
    lines[...] = total.reshape(slots * 16, LANES)
    outputs = []
    for k in range(8):
        outputs.append(lines[pl.ds(k, slots, stride=16), :].astype(BF16))
        slot_grads[:, k * LANES : (k + 1) * LANES] = lines[pl.ds(8 + k, slots, stride=16), :].astype(BF16)
    c = combine[...]
    g = dot(jnp.concatenate(outputs, axis=1), grads[...], ((1,), (1,)))
    change = c * (g - jnp.sum(c * g, axis=0, keepdims=True))
    d = dispatch[...]
    g = dot(slot_grads[...], tokens[...], ((1,), (1,)))
    change = change + d * (g - jnp.sum(d * g, axis=1, keepdims=True))
    change = change.astype(BF16)
    logit_grads[...] = change
    term = dot(change, tokens[...], ((1,), (0,)))
    for h in range(2):
        for i in range(slots // 16):
            for k in range(width // LANES):
                for a in range(4):
                    row = h * (slots // 2) + i * 8 + a * 2
                    halves[h, (i * (width // LANES) + k) * 4 + a] = term[
                        row : row + 2, k * LANES : (k + 1) * LANES
                    ]
    kept[...] = halves[core[0]]
    sent[...] = halves[1 - core[0]]


def image_kernel(dispatch, logit_grads, slot_grads, param, grad_image):
    left = jnp.concatenate([dispatch[...].astype(BF16), logit_grads[...]], axis=0)
    right = jnp.concatenate([slot_grads[...], param[...]], axis=0)
    grad_image[...] = dot(left, right, ((0,), (0,))).astype(BF16)


def sum_kernel(blocks, out):
    total = jnp.sum(blocks[...], axis=0, keepdims=True)
    out[...] = jnp.broadcast_to(total, out.shape)


def last_kernel(core, half, other, out):
    slots, width = out.shape
    for source, which in ((half, core[0]), (other, 1 - core[0])):
        for i in range(slots // 16):
            for k in range(width // LANES):
                tile = [source[(i * (width // LANES) + k) * 4 + a] for a in range(4)]
                row = pl.multiple_of(which * (slots // 2) + i * 8, 8)
                out[pl.ds(row, 8), k * LANES : (k + 1) * LANES] = jnp.concatenate(tile, axis=0)


def shards(tokens, slot_param, up_weight, down_weight, grad_output):
    image_tokens = tokens[0]
    image_grads = grad_output[0]
    up = up_weight[0]
    down = down_weight[0]
    count, width = image_tokens.shape
    hidden = up.shape[1]
    chips = lax.axis_size(CHIPS)
    copies = lax.axis_size("y_hi")
    slots = slot_param.shape[1]
    core = lax.axis_index("core").astype(jnp.int32).reshape(1)
    param = slot_param.T
    rows, dispatch, combine = call(
        front_kernel,
        [((slots, copies, 16, LANES), BF16), ((slots, count), F32), ((slots, count), F32)],
        [((slots * 16, LANES), F32)],
        flops=6 * slots * count * width,
        moved=6 * count * width,
    )(image_tokens, image_grads, param)
    mine = exchange(rows.reshape(chips, 16, LANES))
    theirs = swap_cores(mine)
    own, send, active, grad_pre, rows_in, rows_grad = call(
        expert_kernel,
        [((chips, 16, LANES), F32), ((chips, 16, LANES), BF16)]
        + [((2 * chips, hidden), BF16)] * 2
        + [((2 * chips, width), BF16)] * 2,
        [((2 * chips * 16, LANES), F32)],
        flops=16 * chips * width * hidden,
        moved=6 * width * hidden,
    )(mine, theirs, up, down)
    summed = (own + swap_cores(send).astype(F32)).astype(BF16)
    returned = exchange(summed)
    grad_up, grad_down = weight_grads(rows_in, grad_pre, active, rows_grad)
    returned, grad_up, grad_down = lax.optimization_barrier((returned, grad_up, grad_down))
    half_shape = (chips, slots * width // 2 // chips // LANES, LANES)
    logit_grads, slot_grads, kept, sent = call(
        back_kernel,
        [((slots, count), BF16), ((slots, width), BF16), (half_shape, F32), (half_shape, F32)],
        [((slots * 16, LANES), F32), ((2,) + half_shape, F32)],
        flops=6 * slots * count * width,
        moved=6 * count * width,
        scalars=1,
    )(core, returned.reshape(slots, copies, 16, LANES), image_tokens, image_grads, dispatch, combine)
    blocks = exchange(kept + swap_cores(sent))
    (grad_image,) = call(
        image_kernel,
        [((count, width), BF16)],
        flops=4 * slots * count * width,
        moved=4 * count * width,
    )(dispatch, logit_grads, slot_grads, param)
    blocks, grad_image = lax.optimization_barrier((blocks, grad_image))
    (block,) = call(sum_kernel, [(half_shape, F32)])(blocks)
    half = exchange(block)
    (param_grad,) = call(last_kernel, [((slots, width), F32)], scalars=1)(core, half, swap_cores(half))
    return (grad_image[None], param_grad.T, grad_up[None], grad_down[None])


def solution(mesh):
    devices = mesh.devices.reshape(4, 2, 8, 2, 2)
    cut = Mesh(devices, ("x", "y_lo", "z", "y_hi", "core"))
    return jax.shard_map(
        shards,
        mesh=cut,
        in_specs=(
            P(EXPERT + DP, None, None),
            P(),
            P(EXPERT, None, DP),
            P(EXPERT, DP, None),
            P(EXPERT + DP, None, None),
        ),
        out_specs=(
            P(EXPERT + DP, None, None),
            P(),
            P(EXPERT, None, DP),
            P(EXPERT, DP, None),
        ),
        check_vma=False,
    )
```

time: 144 us -> 124 us (0.86)
  matrix products: 19.6 us -> 0 us
  Pallas kernels: 0 us -> 11.7 us
  other arithmetic: 7.68 us -> 1.62 us
  local copies, waits for them, and re-layouts: 13.1 us -> 10.6 us
    dot_general x13 -> x0, matrix products: 19.6 us -> none  [dot(): lax.dot_general(a, b, (dims, ((), ())), preferred_element_type=jnp.float32)]
    pallas_call x0 -> x7, Pallas kernels: none -> 11.7 us  [the longest x6 8.47 us: run(): pl.pallas_call(kernel, out_shape=[jax.ShapeDtypeStruct(shape, dtype) for...]
    unnamed x29 -> x28, local copies, waits for them, and re-layouts: 2.09 us -> 10.6 us
    reshape x3 -> x0, local copies, waits for them, and re-layouts: 3.74 us -> none  [the longest x1 1.96 us: shards(): returned = exchange(summed.astype(bf16)).reshape(slots, copies, 2, width)]
    all_to_all x2, waiting for transfers between devices: 23 us -> 20 us  [exchange(): return lax.all_to_all(blocks, CHIPS, 0, 0, tiled=True)]
    convert_element_type x2 -> x0, local copies, waits for them, and re-layouts: 2.5 us -> none  [the longest x1 1.31 us: shards(): partial[0].astype(jnp.float32) + swap_cores(partial[1]).astype(jnp.float32)]
    slice x2 -> x0, local copies, waits for them, and re-layouts: 2.41 us -> none  [the longest x1 2.04 us: shards(): partial[1]]
    reduce_sum x3 -> x0, other arithmetic: 2.24 us -> none  [the longest x1 1.89 us: shards(): returned = jnp.sum(returned.astype(jnp.float32), axis=1).astype(bf16)]
  transfers between devices with their start and end apart: 6 -> 6, of which waited for: 5 -> 6; matrix products, arithmetic and copies ran while one was open for 7% -> 0% of each run, Pallas kernels for 0% -> 4%
where the time goes in v2:
time: 124 us; the launch traced here: 123 us
  blocking collectives  49.7 us (40%)
  waiting for transfers between devices  25.1 us (20%)
  starting transfers between devices  23.9 us (19%)
  Pallas kernels  11.7 us (9%)
  local copies, waits for them, and re-layouts  10.6 us (9%)
  other arithmetic  1.62 us (1%)
    all_to_all x2, blocking collectives, exchange(): return lax.all_to_all(blocks, CHIPS, 0, 0, tiled=True)  49.7 us
    all_to_all x2, waiting for transfers between devices, exchange(): return lax.all_to_all(blocks, CHIPS, 0, 0, tiled=True)  20 us
    all_to_all x2, starting transfers between devices, exchange(): return lax.all_to_all(blocks, CHIPS, 0, 0, tiled=True)  14 us
    unnamed x28, local copies, waits for them, and re-layouts  10.6 us
    ppermute x4, starting transfers between devices, swap_cores(): return lax.ppermute(values, 'core', [(0, 1), (1, 0)])  9.96 us
    pallas_call x6, Pallas kernels, run(): pl.pallas_call(kernel, out_shape=[jax.ShapeDtypeStruct(shape, dtype) for...  8.47 us
    ppermute x4, waiting for transfers between devices, swap_cores(): return lax.ppermute(values, 'core', [(0, 1), (1, 0)])  5.05 us
    pallas_call x1, Pallas kernels, weight_grads(): pl.pallas_call(weights_kernel, grid=(width // step,), out_shape=[jax.Shap...  3.18 us
  transfers between devices with their start and end apart: 6, of which 6 were waited for; matrix products, arithmetic and copies ran while one was open for 0% of the time, Pallas kernels for 4%

profile of v2, /device:TPU:1, one launch (start us, length us, event | category | flops | bytes accessed | tf_op | source)
XLA Modules:
  0.0 123.3 jit_solution(1692008295475564037)
XLA Ops:
  0.6 1.2 copy-done
  1.9 1.2 copy-done.2
  3.1 0.9 copy-done.4
  4.0 1.1 shard_map.84
  5.1 32.6 %all_to_all.20.mine = bf16[128,16,128]{2,1,0:T(8,128)(2,1)S(1)} all-to-all(bf16[128,16,128]{2,1,0:T(8,128)(2,1)S(1)} %bitcast.19), channel_id=1, replica_groups=mesh['x'=4,'y_lo'=2,'z'=8,'y_hi'=2,'core'=2] {'x','y_lo','z','y_hi'}, dimensions={0} | all-to-all | bytes 1048576 | tf_op jit(solution)/shard_map/all_to_all | solution.py:30
  37.7 3.7 %collective-permute-start = (bf16[128,16,128]{2,1,0:T(8,128)(2,1)S(1)}, bf16[128,16,128]{2,1,0:T(8,128)(2,1)S(1)}, u32[]{:S(2)}, u32[]{:S(2)}) collective-permute-start(bf16[128,16,128]{2,1,0:T(8,128)(2,1)S(1)} %all_to_all.20.mine), channel_id=1, source_target_pairs={{0,1},{1,0},{2,3},{3,2},{4,5},{5,4},{6,7},{7,6},{8,9},{9,8},{10,11... | collective-permute-start | bytes 1572872 | tf_op jit(solution)/shard_map/ppermute | solution.py:26
  41.5 1.5 %collective-permute-done.theirs = bf16[128,16,128]{2,1,0:T(8,128)(2,1)S(1)} collective-permute-done((bf16[128,16,128]{2,1,0:T(8,128)(2,1)S(1)}, bf16[128,16,128]{2,1,0:T(8,128)(2,1)S(1)}, u32[]{:S(2)}, u32[]{:S(2)}) %collective-permute-start) | collective-permute-done | bytes 524320 | tf_op jit(solution)/shard_map/ppermute | solution.py:26
  43.0 1.6 %copy-done.7 = bf16[1,1024,1024]{2,1,0:T(8,128)(2,1)S(1)} copy-done((bf16[1,1024,1024]{2,1,0:T(8,128)(2,1)S(1)}, bf16[1,1024,1024]{2,1,0:T(8,128)(2,1)}, u32[]{:S(2)}) %copy-start.7) | copy-done | bytes 2097176
  44.6 3.8 %shard_map.85 = (f32[128,16,128]{2,1,0:T(8,128)S(1)}, bf16[128,16,128]{2,1,0:T(8,128)(2,1)S(1)}, bf16[256,1024]{1,0:T(8,128)(2,1)S(1)}, bf16[256,1024]{1,0:T(8,1...) custom-call(bf16[128,16,128]{2,1,0:T(8,128)(2,1)S(1)} %all_to_all.20.mine, ...), custom_call_target="tpu_custom_call" | custom-call | flops 2147483648 | bytes 6291456 | tf_op jit(solution)/shard_map/pallas_call | solution.py:39
  48.4 0.8 copy-done.8
  49.2 0.8 copy-done.10
  50.0 0.8 copy-done.12
  50.8 0.4 collective-permute-start.1
  51.2 1.5 %collective-permute-done.1 = bf16[128,16,128]{2,1,0:T(8,128)(2,1)S(1)} collective-permute-done((bf16[128,16,128]{2,1,0:T(8,128)(2,1)S(1)}, bf16[128,16,128]{2,1,0:T(8,128)(2,1)S(1)}, u32[]{:S(2)}, u32[]{:S(2)}) %collective-permute-start.1) | collective-permute-done | bytes 524320 | tf_op jit(solution)/shard_map/ppermute | solution.py:26
  52.7 0.9 add_convert_fusion
  53.6 6.9 %all-to-all-start.1 = ((bf16[128,16,128]{2,1,0:T(8,128)(2,1)}), bf16[128,16,128]{2,1,0:T(8,128)(2,1)S(1)}, u32[]{:S(2)}, u32[]{:S(2)}) async-start(bf16[128,16,128]{2,1,0:T(8,128)(2,1)} %add_convert_fusion), calls=%async_computation.1 | async-start | bytes 1048576 | tf_op jit(solution)/shard_map/all_to_all | solution.py:30
  60.5 1.2 copy-done.9
  61.7 1.0 copy-done.11
  62.7 1.0 copy-done.13
  63.8 3.2 %shard_map.86 = (bf16[1024,1024]{1,0:T(8,128)(2,1)}, bf16[1024,1024]{1,0:T(8,128)(2,1)}) custom-call(bf16[256,1024]{1,0:T(8,128)(2,1)S(1)} %copy-done.11, bf16[256,1024]{1,0:T(8,128)(2,1)S(1)} %copy-done.9, bf16[256,1024]{1,0:T(8,128)(2,1)S(1)} %get-tuple-element.29.active, bf16[256,1024]{1,0:T(8,128)(2,1)S(1)} %copy-done.13), custom_call_target="tpu_custom_call" | custom-call | flops 1073741824 | bytes 4194304 | tf_op jit(solution)/shard_map/pallas_call | solution.py:113
  67.0 10.4 %all-to-all-done.1 = bf16[128,16,128]{2,1,0:T(8,128)(2,1)S(1)} async-done(((bf16[128,16,128]{2,1,0:T(8,128)(2,1)}), bf16[128,16,128]{2,1,0:T(8,128)(2,1)S(1)}, u32[]{:S(2)}, u32[]{:S(2)}) %all-to-all-start.1) | async-done | bytes 524320 | tf_op jit(solution)/shard_map/all_to_all | solution.py:30
  77.4 1.2 shard_map.87
  78.6 3.3 %collective-permute-start.2 = (f32[128,2,128]{2,1,0:T(2,128)S(1)}, f32[128,2,128]{2,1,0:T(2,128)S(1)}, u32[]{:S(2)}, u32[]{:S(2)}) collective-permute-start(f32[128,2,128]{2,1,0:T(2,128)S(1)} %get-tuple-element.37), channel_id=1, source_target_pairs={{0,1},{1,0},{2,3},{3,2},{4,5},{5,4},{6,7},{7,6},{8,9},{9,8},{10,11... | collective-permute-start | bytes 393224 | tf_op jit(solution)/shard_map/ppermute | solution.py:26
  81.9 1.0 collective-permute-done.2
  82.9 0.7 add.7
  83.6 7.1 %all-to-all-start.2 = ((f32[128,2,128]{2,1,0:T(2,128)}), f32[128,2,128]{2,1,0:T(2,128)S(1)}, u32[]{:S(2)}, u32[]{:S(2)}) async-start(f32[128,2,128]{2,1,0:T(2,128)} %add.7), calls=%async_computation.2 | async-start | bytes 262144 | tf_op jit(solution)/shard_map/all_to_all | solution.py:30
  90.7 1.4 %shard_map.88 = bf16[512,1024]{1,0:T(8,128)(2,1)} custom-call(f32[64,512]{1,0:T(8,128)S(1)} %get-tuple-element.34.dispatch, bf16[64,512]{1,0:T(8,128)(2,1)S(1)} %get-tuple-element.38.logit_grads, bf16[64,1024]{1,0:T(8,128)(2,1)S(1)} %get-tuple-element.39.slot_grads, bf16[64,1024]{1,0:T(8,128)(2,1)S(1)} %bitcast.18), custom_call_target="tpu_custom_call" | custom-call | flops 134217728 | bytes 2097152 | tf_op jit(solution)/shard_map/pallas_call | solution.py:39
  92.2 9.6 %all-to-all-done.2.blocks = f32[128,2,128]{2,1,0:T(2,128)S(1)} async-done(((f32[128,2,128]{2,1,0:T(2,128)}), f32[128,2,128]{2,1,0:T(2,128)S(1)}, u32[]{:S(2)}, u32[]{:S(2)}) %all-to-all-start.2) | async-done | bytes 131104 | tf_op jit(solution)/shard_map/all_to_all | solution.py:30
  101.9 17.1 %all_to_all.21.half = f32[128,2,128]{2,1,0:T(2,128)S(1)} all-to-all(f32[128,2,128]{2,1,0:T(2,128)S(1)} %shard_map.89), channel_id=1, replica_groups=mesh['x'=4,'y_lo'=2,'z'=8,'y_hi'=2,'core'=2] {'x','y_lo','z','y_hi'}, dimensions={0} | all-to-all | bytes 262144 | tf_op jit(solution)/shard_map/all_to_all | solution.py:30
  119.0 2.6 %collective-permute-start.3 = (f32[128,2,128]{2,1,0:T(2,128)S(1)}, f32[128,2,128]{2,1,0:T(2,128)S(1)}, u32[]{:S(2)}, u32[]{:S(2)}) collective-permute-start(f32[128,2,128]{2,1,0:T(2,128)S(1)} %all_to_all.21.half), channel_id=1, source_target_pairs={{0,1},{1,0},{2,3},{3,2},{4,5},{5,4},{6,7},{7,6},{8,9},{9,8},{10,11... | collective-permute-start | bytes 393224 | tf_op jit(solution)/shard_map/ppermute | solution.py:26
  121.6 1.0 collective-permute-done.3.other
  122.6 0.8 shard_map.90
  (19 shorter events, 0.2 us)
Async XLA Ops:
  0.6 1.2 copy-start
  1.9 1.2 copy-start.2
  3.1 0.9 copy-start.4
  4.0 39.0 %copy-start.6 = (bf16[1,1024,1024]{2,1,0:T(8,128)(2,1)S(1)}, bf16[1,1024,1024]{2,1,0:T(8,128)(2,1)}, u32[]{:S(2)}) copy-start(bf16[1,1024,1024]{2,1,0:T(8,128)(2,1)} %param.7) | copy-start | bytes 6291460
  37.7 5.3 %collective-permute-start = (bf16[128,16,128]{2,1,0:T(8,128)(2,1)S(1)}, bf16[128,16,128]{2,1,0:T(8,128)(2,1)S(1)}, u32[]{:S(2)}, u32[]{:S(2)}) collective-permute-start(bf16[128,16,128]{2,1,0:T(8,128)(2,1)S(1)} %all_to_all.20.mine), channel_id=1, source_target_pairs={{0,1},{1,0},{2,3},{3,2},{4,5},{5,4},{6,7},{7,6},{8,9},{9,8},{10,11... | collective-permute-start | bytes 1572872 | tf_op jit(solution)/shard_map/ppermute | solution.py:26
  43.0 1.6 %copy-start.7 = (bf16[1,1024,1024]{2,1,0:T(8,128)(2,1)S(1)}, bf16[1,1024,1024]{2,1,0:T(8,128)(2,1)}, u32[]{:S(2)}) copy-start(bf16[1,1024,1024]{2,1,0:T(8,128)(2,1)} %param.8) | copy-start | bytes 6291460
  48.4 0.8 copy-start.8
  49.2 0.8 copy-start.10
  50.0 0.8 copy-start.12
  50.8 1.9 %collective-permute-start.1 = (bf16[128,16,128]{2,1,0:T(8,128)(2,1)S(1)}, bf16[128,16,128]{2,1,0:T(8,128)(2,1)S(1)}, u32[]{:S(2)}, u32[]{:S(2)}) collective-permute-start(bf16[128,16,128]{2,1,0:T(8,128)(2,1)S(1)} %get-tuple-element.26), channel_id=1, source_target_pairs={{0,1},{1,0},{2,3},{3,2},{4,5},{5,4},{6,7},{7,6},{8,9},{9,8},{10,11... | collective-permute-start | bytes 1572872 | tf_op jit(solution)/shard_map/ppermute | solution.py:26
  53.6 23.8 %all-to-all-start.1 = ((bf16[128,16,128]{2,1,0:T(8,128)(2,1)}), bf16[128,16,128]{2,1,0:T(8,128)(2,1)S(1)}, u32[]{:S(2)}, u32[]{:S(2)}) async-start(bf16[128,16,128]{2,1,0:T(8,128)(2,1)} %add_convert_fusion), calls=%async_computation.1 | async-start | bytes 1048576 | tf_op jit(solution)/shard_map/all_to_all | solution.py:30
  60.5 16.9 %copy-start.1 = (bf16[1,512,1024]{2,1,0:T(8,128)(2,1)S(1)}, bf16[1,512,1024]{2,1,0:T(8,128)(2,1)}, u32[]{:S(2)}) copy-start(bf16[1,512,1024]{2,1,0:T(8,128)(2,1)} %param.5) | copy-start | bytes 3145732
  60.5 16.9 %copy-start.3 = (bf16[1,512,1024]{2,1,0:T(8,128)(2,1)S(1)}, bf16[1,512,1024]{2,1,0:T(8,128)(2,1)}, u32[]{:S(2)}) copy-start(bf16[1,512,1024]{2,1,0:T(8,128)(2,1)} %param.9) | copy-start | bytes 3145732
  60.5 1.2 copy-start.9
  61.7 1.0 copy-start.11
  62.7 1.0 copy-start.13
  67.0 23.8 %copy-start.5 = (bf16[1024,64]{0,1:T(8,128)(2,1)S(1)}, bf16[1024,64]{0,1:T(8,128)(2,1)}, u32[]{:S(2)}) copy-start(bf16[1024,64]{0,1:T(8,128)(2,1)} %param.6) | copy-start | bytes 393220
  78.6 4.3 %collective-permute-start.2 = (f32[128,2,128]{2,1,0:T(2,128)S(1)}, f32[128,2,128]{2,1,0:T(2,128)S(1)}, u32[]{:S(2)}, u32[]{:S(2)}) collective-permute-start(f32[128,2,128]{2,1,0:T(2,128)S(1)} %get-tuple-element.37), channel_id=1, source_target_pairs={{0,1},{1,0},{2,3},{3,2},{4,5},{5,4},{6,7},{7,6},{8,9},{9,8},{10,11... | collective-permute-start | bytes 393224 | tf_op jit(solution)/shard_map/ppermute | solution.py:26
  83.6 18.1 %all-to-all-start.2 = ((f32[128,2,128]{2,1,0:T(2,128)}), f32[128,2,128]{2,1,0:T(2,128)S(1)}, u32[]{:S(2)}, u32[]{:S(2)}) async-start(f32[128,2,128]{2,1,0:T(2,128)} %add.7), calls=%async_computation.2 | async-start | bytes 262144 | tf_op jit(solution)/shard_map/all_to_all | solution.py:30
  119.0 3.5 %collective-permute-start.3 = (f32[128,2,128]{2,1,0:T(2,128)S(1)}, f32[128,2,128]{2,1,0:T(2,128)S(1)}, u32[]{:S(2)}, u32[]{:S(2)}) collective-permute-start(f32[128,2,128]{2,1,0:T(2,128)S(1)} %all_to_all.21.half), channel_id=1, source_target_pairs={{0,1},{1,0},{2,3},{3,2},{4,5},{5,4},{6,7},{7,6},{8,9},{9,8},{10,11... | collective-permute-start | bytes 393224 | tf_op jit(solution)/shard_map/ppermute | solution.py:26

commit v3 on v2

v3 whole, which is shorter than its diff:
```python
import jax
import jax.numpy as jnp
from jax import lax
from jax.experimental import pallas as pl
from jax.experimental.pallas import tpu as pltpu
from jax.sharding import Mesh, PartitionSpec as P

gelu_coeff = 0.7978845608
cubic_coeff = 0.044715

CHIPS = ("x", "y_lo", "z", "y_hi")
EXPERT = ("x", "y_lo", "z")
DP = ("y_hi", "core")
F32 = jnp.float32
BF16 = jnp.bfloat16
LANES = 128


def dot(a, b, dims):
    return lax.dot_general(a, b, (dims, ((), ())), preferred_element_type=F32)


def swap_cores(values):
    return lax.ppermute(values, "core", [(0, 1), (1, 0)])


def exchange(blocks):
    return lax.all_to_all(blocks, CHIPS, 0, 0, tiled=True)


def call(kernel, outs, scratch=(), flops=0, moved=0, hbm=(), hbm_outs=(), limit=4):
    def shape_of(i, shape, dtype):
        if hbm_outs is None:
            return jax.ShapeDtypeStruct(shape, dtype)
        return pltpu.HBM(shape, dtype) if i in hbm_outs else pltpu.VMEM(shape, dtype)

    kept = () if hbm_outs is None else hbm_outs

    def run(*args):
        args = [pltpu.with_memory_space_constraint(x, pltpu.HBM) if i in hbm else x for i, x in enumerate(args)]
        return pl.pallas_call(
            kernel,
            out_shape=[shape_of(i, shape, dtype) for i, (shape, dtype) in enumerate(outs)],
            in_specs=[pl.BlockSpec(memory_space=pltpu.HBM if i in hbm else pltpu.VMEM) for i in range(len(args))],
            out_specs=[pl.BlockSpec(memory_space=pltpu.HBM if i in kept else pltpu.VMEM) for i in range(len(outs))],
            scratch_shapes=list(scratch),
            compiler_params=pltpu.CompilerParams(vmem_limit_bytes=limit << 20),
            cost_estimate=pl.CostEstimate(flops=flops, bytes_accessed=moved, transcendentals=0),
        )(*args)

    return run


def to_blocks(scratch, values, first, rows, start=0):
    for k in range(values.shape[1] // LANES):
        scratch[pl.ds(start + first + k, rows, stride=16), :] = values[:, k * LANES : (k + 1) * LANES]


PIECES = 4


def front_kernel(tokens_in, grads_in, param_in, up_in, down_in, rows, dispatch, combine, tokens, grads, up, down, param, lines, sems):
    slots, width = param.shape
    count = tokens.shape[0]
    piece = count // PIECES
    copies = [pltpu.make_async_copy(param_in, param, sems.at[2 * PIECES])]
    for j, (source, target) in enumerate(((tokens_in, tokens), (grads_in, grads))):
        for p in range(PIECES):
            part = pl.ds(p * piece, piece)
            copies.append(pltpu.make_async_copy(source.at[part], target.at[part], sems.at[j * PIECES + p]))
    copies.append(pltpu.make_async_copy(up_in, up, sems.at[2 * PIECES + 1]))
    copies.append(pltpu.make_async_copy(down_in, down, sems.at[2 * PIECES + 2]))
    for copy in copies:
        copy.start()
    copies[0].wait()
    logits = []
    for p in range(PIECES):
        copies[1 + p].wait()
        logits.append(dot(param[...], tokens[p * piece : (p + 1) * piece, :], ((1,), (1,))))
    logits = jnp.concatenate(logits, axis=1)
    e = jnp.exp(logits - jnp.max(logits, axis=1, keepdims=True))
    d = e / jnp.sum(e, axis=1, keepdims=True)
    e = jnp.exp(logits - jnp.max(logits, axis=0, keepdims=True))
    c = e / jnp.sum(e, axis=0, keepdims=True)
    dispatch[...] = d
    combine[...] = c
    to_blocks(lines, dot(d.astype(BF16), tokens[...], ((1,), (0,))), 0, slots)
    for p in range(PIECES):
        copies[1 + PIECES + p].wait()
    to_blocks(lines, dot(c.astype(BF16), grads[...], ((1,), (0,))), 8, slots)
    blocks = lines[...].reshape(slots, 16, LANES).astype(BF16)
    for copy in range(rows.shape[1]):
        rows[:, copy] = blocks
    for copy in copies[1 + 2 * PIECES :]:
        copy.wait()


def expert_kernel(mine, up_own, up_other, down_own, down_other, back, keep, swap, parts, lines, sems):
    images = mine.shape[0]
    width, hidden = up_own.shape
    blocks = mine[...]
    parts[0] = blocks[:, :8].reshape(images, width)
    parts[1] = blocks[:, 8:].reshape(images, width)
    targets = [swap.at[j] for j in range(4)] + [keep.at[j] for j in range(2)]
    copies = [pltpu.make_async_copy(parts.at[j], targets[j], sems.at[j]) for j in range(6)]
    copies[0].start()
    copies[1].start()
    rows_in = parts[0]
    rows_grad = parts[1]
    for up, down, first in ((up_other, down_other, 2), (up_own, down_own, 4)):
        for c in range(0, hidden, 256):
            cols = slice(c, c + 256)
            v = dot(rows_in, up[:, cols], ((1,), (0,)))
            tangent = jnp.tanh(gelu_coeff * (v + cubic_coeff * v * v * v))
            parts[first, :, cols] = (0.5 * v * (1.0 + tangent)).astype(BF16)
            slope = 0.5 * (1.0 + tangent) + 0.5 * v * (1.0 - tangent * tangent) * gelu_coeff * (
                1.0 + 3.0 * cubic_coeff * v * v
            )
            g = dot(rows_grad, down[cols, :], ((1,), (1,)))
            parts[first + 1, :, cols] = (g * slope).astype(BF16)
        copies[first].start()
        copies[first + 1].start()
    for n in range(0, width, 256):
        cols = slice(n, n + 256)
        out = dot(parts[4], down_own[:, cols], ((1,), (0,))) + dot(parts[2], down_other[:, cols], ((1,), (0,)))
        to_blocks(lines, out, n // LANES, images)
        out = dot(parts[5], up_own[cols, :], ((1,), (1,))) + dot(parts[3], up_other[cols, :], ((1,), (1,)))
        to_blocks(lines, out, 8 + n // LANES, images)
    back[...] = lines[...].reshape(images, 16, LANES).astype(BF16)
    for copy in copies:
        copy.wait()


def weights_kernel(keep, swap, recv, grad_up, grad_down):
    step = grad_up.shape[0]
    cols = pl.ds(pl.multiple_of(pl.program_id(0) * step, step), step)
    both = lambda a, b: jnp.concatenate([a, b], axis=0)
    rows_in = both(swap[0, :, cols], recv[0, :, cols])
    grad_up[...] = dot(rows_in, both(keep[1], recv[3]), ((0,), (0,))).astype(BF16)
    active = both(keep[0, :, cols], recv[2, :, cols])
    grad_down[...] = dot(active, both(swap[1], recv[1]), ((0,), (0,))).astype(BF16)


def weight_grads(keep, swap, recv):
    images, width = swap.shape[1:]
    step = 256
    whole = lambda n: pl.BlockSpec((n, images, width), lambda i: (0, 0, 0))
    return pl.pallas_call(
        weights_kernel,
        grid=(width // step,),
        out_shape=[jax.ShapeDtypeStruct((width, width), BF16)] * 2,
        in_specs=[whole(2), whole(4), whole(4)],
        out_specs=[pl.BlockSpec((step, width), lambda i: (i, 0))] * 2,
        compiler_params=pltpu.CompilerParams(vmem_limit_bytes=12 << 20),
        cost_estimate=pl.CostEstimate(
            flops=8 * images * width * width, bytes_accessed=4 * width * width, transcendentals=0
        ),
    )(keep, swap, recv)


def back_kernel(returned, tokens, grads, dispatch, combine, logit_grads, slot_grads, blocks, lines):
    slots = logit_grads.shape[0]
    width = tokens.shape[1]
    total = returned[:, 0].astype(F32)
    for copy in range(1, returned.shape[1]):
        total = total + returned[:, copy].astype(F32)
    lines[...] = total.reshape(slots * 16, LANES)
    outputs = []
    for k in range(width // LANES):
        outputs.append(lines[pl.ds(k, slots, stride=16), :].astype(BF16))
        slot_grads[:, k * LANES : (k + 1) * LANES] = lines[pl.ds(8 + k, slots, stride=16), :].astype(BF16)
    c = combine[...]
    g = dot(jnp.concatenate(outputs, axis=1), grads[...], ((1,), (1,)))
    change = c * (g - jnp.sum(c * g, axis=0, keepdims=True))
    d = dispatch[...]
    g = dot(slot_grads[...], tokens[...], ((1,), (1,)))
    change = change + d * (g - jnp.sum(d * g, axis=1, keepdims=True))
    change = change.astype(BF16)
    logit_grads[...] = change
    term = dot(change, tokens[...], ((1,), (0,)))
    for first, row, col in tiles(slots, width):
        blocks[first : first + 16, :] = term[row : row + 16, col : col + LANES].astype(BF16)


def tiles(slots, width):
    first = 0
    for row in range(0, slots, 16):
        for col in range(0, width, LANES):
            yield first, row, col
            first += 16


def image_kernel(dispatch, logit_grads, slot_grads, param, grad_image):
    left = jnp.concatenate([dispatch[...].astype(BF16), logit_grads[...]], axis=0)
    right = jnp.concatenate([slot_grads[...], param[...]], axis=0)
    grad_image[...] = dot(left, right, ((0,), (0,))).astype(BF16)


def add_kernel(a, b, out):
    out[...] = a[...] + b[...]


def sum_kernel(blocks, out):
    rows = out.shape[0]
    total = jnp.sum(blocks[...].astype(F32).reshape(-1, 8, LANES), axis=0)
    out[...] = sum(total[i : i + rows] for i in range(0, 8, rows))


def spread_kernel(a, b, out):
    total = a[...] + b[...]
    tile = jnp.concatenate([total] * (16 // total.shape[0]), axis=0).astype(BF16)
    for first in range(0, out.shape[0], 16):
        out[first : first + 16, :] = tile


def last_kernel(blocks, out):
    for first, row, col in tiles(*out.shape):
        out[row : row + 16, col : col + LANES] = blocks[first : first + 16, :].astype(F32)


def shards(tokens, slot_param, up_weight, down_weight, grad_output):
    image_tokens = tokens[0]
    image_grads = grad_output[0]
    up = up_weight[0]
    down = down_weight[0]
    count, width = image_tokens.shape
    hidden = up.shape[1]
    chips = lax.axis_size(CHIPS)
    copies = lax.axis_size("y_hi")
    slots = slot_param.shape[1]
    param = slot_param.T
    up_other = swap_cores(up)
    down_other = swap_cores(down)
    rows, dispatch, combine, image_tokens, image_grads, up_own, down_own = call(
        front_kernel,
        [((slots, copies, 16, LANES), BF16), ((slots, count), F32), ((slots, count), F32)]
        + [((count, width), BF16)] * 2
        + [((width, hidden), BF16), ((hidden, width), BF16)],
        [
            pltpu.VMEM((slots, width), BF16),
            pltpu.VMEM((slots * 16, LANES), F32),
            pltpu.SemaphoreType.DMA((2 * PIECES + 3,)),
        ],
        flops=6 * slots * count * width,
        moved=16 * width * hidden,
        hbm=(0, 1, 2, 3, 4),
    )(image_tokens, image_grads, param, up, down)
    mine = exchange(rows.reshape(chips, 16, LANES))
    back, keep, swap = call(
        expert_kernel,
        [((chips, 16, LANES), BF16), ((2, chips, width), BF16), ((4, chips, width), BF16)],
        [
            pltpu.VMEM((6, chips, width), BF16),
            pltpu.VMEM((chips * 16, LANES), F32),
            pltpu.SemaphoreType.DMA((6,)),
        ],
        flops=16 * chips * width * hidden,
        moved=4 * width * hidden,
        hbm_outs=(1, 2),
        limit=8,
    )(mine, up_own, up_other, down_own, down_other)
    returned = exchange(back)
    lines = slots * width // LANES
    logit_grads, slot_grads, blocks = call(
        back_kernel,
        [((slots, count), BF16), ((slots, width), BF16), ((lines, LANES), BF16)],
        [pltpu.VMEM((slots * 16, LANES), F32)],
        flops=6 * slots * count * width,
        moved=6 * count * width,
    )(returned.reshape(slots, copies, 16, LANES), image_tokens, image_grads, dispatch, combine)
    blocks = exchange(blocks.reshape(chips, lines // chips, LANES)).reshape(lines, LANES)
    (block,) = call(sum_kernel, [((lines // chips, LANES), F32)])(blocks)
    block, other, keep, swap, logit_grads, slot_grads = lax.optimization_barrier(
        (block, swap_cores(block), keep, swap, logit_grads, slot_grads)
    )
    recv = swap_cores(swap)
    (blocks,) = call(spread_kernel, [((lines, LANES), BF16)])(block, other)
    blocks = exchange(blocks.reshape(chips, lines // chips, LANES)).reshape(lines, LANES)
    grad_up, grad_down = weight_grads(keep, swap, recv)
    (grad_image,) = call(
        image_kernel,
        [((count, width), BF16)],
        flops=4 * slots * count * width,
        moved=4 * count * width,
        hbm_outs=None,
    )(dispatch, logit_grads, slot_grads, param)
    blocks, grad_image, grad_up, grad_down = lax.optimization_barrier((blocks, grad_image, grad_up, grad_down))
    (param_grad,) = call(last_kernel, [((slots, width), F32)], hbm_outs=None)(blocks)
    return (grad_image[None], param_grad.T, grad_up[None], grad_down[None])


def solution(mesh):
    devices = mesh.devices.reshape(4, 2, 8, 2, 2)
    cut = Mesh(devices, ("x", "y_lo", "z", "y_hi", "core"))
    return jax.shard_map(
        shards,
        mesh=cut,
        in_specs=(
            P(EXPERT + DP, None, None),
            P(),
            P(EXPERT, None, DP),
            P(EXPERT, DP, None),
            P(EXPERT + DP, None, None),
        ),
        out_specs=(
            P(EXPERT + DP, None, None),
            P(),
            P(EXPERT, None, DP),
            P(EXPERT, DP, None),
        ),
        check_vma=False,
    )
```

time: 124 us -> 112 us (0.903)
  blocking collectives: 49.7 us -> 75 us
  waiting for transfers between devices: 25.1 us -> 7.54 us
  local copies, waits for them, and re-layouts: 10.6 us -> 0.01 us
  starting transfers between devices: 23.9 us -> 13.4 us
  Pallas kernels: 11.7 us -> 15 us
  other arithmetic: 1.62 us -> 0 us
    all_to_all x2 -> x3, blocking collectives: 49.7 us -> 75 us  [exchange(): return lax.all_to_all(blocks, CHIPS, 0, 0, tiled=True)]
    all_to_all x2 -> x1, waiting for transfers between devices: 20 us -> 6.71 us  [exchange(): return lax.all_to_all(blocks, CHIPS, 0, 0, tiled=True)]
    unnamed x28 -> x6, local copies, waits for them, and re-layouts: 10.6 us -> 0.01 us
    all_to_all x2 -> x1, starting transfers between devices: 14 us -> 6.17 us  [exchange(): return lax.all_to_all(blocks, CHIPS, 0, 0, tiled=True)]
    ppermute x4, waiting for transfers between devices: 5.05 us -> 0.83 us  [swap_cores(): return lax.ppermute(values, 'core', [(0, 1), (1, 0)])]
    pallas_call x6 -> x7, Pallas kernels: 8.47 us -> 11.9 us  [run(): pl.pallas_call(kernel, out_shape=[shape_of(i, shape, dtype) for i, (shape...]
    ppermute x4, starting transfers between devices: 9.96 us -> 7.26 us  [swap_cores(): return lax.ppermute(values, 'core', [(0, 1), (1, 0)])]
  transfers between devices with their start and end apart: 6 -> 5, of which waited for: 6 -> 2; matrix products, arithmetic and copies ran while one was open for 0% -> 0% of each run, Pallas kernels for 4% -> 7%
where the time goes in v3:
time: 112 us
  blocking collectives  75 us (67%)
  Pallas kernels  15 us (13%)
  starting transfers between devices  13.4 us (12%)
  waiting for transfers between devices  7.54 us (7%)
    all_to_all x3, blocking collectives, exchange(): return lax.all_to_all(blocks, CHIPS, 0, 0, tiled=True)  75 us
    pallas_call x7, Pallas kernels, run(): pl.pallas_call(kernel, out_shape=[shape_of(i, shape, dtype) for i, (shape...  11.9 us
    ppermute x4, starting transfers between devices, swap_cores(): return lax.ppermute(values, 'core', [(0, 1), (1, 0)])  7.26 us
    all_to_all x1, waiting for transfers between devices, exchange(): return lax.all_to_all(blocks, CHIPS, 0, 0, tiled=True)  6.71 us
    all_to_all x1, starting transfers between devices, exchange(): return lax.all_to_all(blocks, CHIPS, 0, 0, tiled=True)  6.17 us
    pallas_call x1, Pallas kernels, weight_grads(): pl.pallas_call(weights_kernel, grid=(width // step,), out_shape=[jax.Shap...  3.11 us
  transfers between devices with their start and end apart: 5, of which 2 were waited for; matrix products, arithmetic and copies ran while one was open for 0% of the time, Pallas kernels for 7%

profile of v3, /device:TPU:1, one launch (start us, length us, event | category | flops | bytes accessed | tf_op | source)
XLA Modules:
  0.0 111.6 jit_solution(11646913713272336435)
XLA Ops:
  0.6 3.3 %collective-permute-start = (bf16[1024,1024]{1,0:T(8,128)(2,1)}, bf16[1024,1024]{1,0:T(8,128)(2,1)S(1)}, u32[]{:S(2)}, u32[]{:S(2)}) collective-permute-start(bf16[1024,1024]{1,0:T(8,128)(2,1)} %bitcast.22), channel_id=1, source_target_pairs={{0,1},{1,0},{2,3},{3,2},{4,5},{5,4},{6,7},{7,6},{8,9},{9,8},{10,11... | collective-permute-start | bytes 6291464 | tf_op jit(solution)/shard_map/ppermute | solution.py:24
  4.0 0.1 collective-permute-start.1
  4.1 3.0 %shard_map.84 = (bf16[64,2,16,128]{3,2,1,0:T(8,128)(2,1)S(1)}, f32[64,512]{1,0:T(8,128)S(1)}, f32[64,512]{1,0:T(8,128)S(1)}, bf16[512,1024]{1,0:T(8,128)(2,1)S(1...) custom-call(bf16[512,1024]{1,0:T(8,128)(2,1)} %bitcast.26, ...), custom_call_target="tpu_custom_call" | custom-call | flops 201326592 | bytes 16777216 | tf_op jit(solution)/shard_map/pallas_call | solution.py:41
  7.1 30.5 %all_to_all.20.mine = bf16[128,16,128]{2,1,0:T(8,128)(2,1)S(1)} all-to-all(bf16[128,16,128]{2,1,0:T(8,128)(2,1)S(1)} %bitcast.19), channel_id=1, replica_groups=mesh['x'=4,'y_lo'=2,'z'=8,'y_hi'=2,'core'=2] {'x','y_lo','z','y_hi'}, dimensions={0} | all-to-all | bytes 1048576 | tf_op jit(solution)/shard_map/all_to_all | solution.py:28
  37.6 0.0 collective-permute-done.up_other
  37.6 0.0 collective-permute-done.1.down_other
  37.6 4.8 %shard_map.85 = (bf16[128,16,128]{2,1,0:T(8,128)(2,1)S(1)}, bf16[2,128,1024]{2,1,0:T(8,128)(2,1)}, bf16[4,128,1024]{2,1,0:T(8,128)(2,1)}) custom-call(bf16[128,16,128]{2,1,0:T(8,128)(2,1)S(1)} %all_to_all.20.mine, bf16[1024,1024]{1,0:T(8,128)(2,1)S(1)} %get-tuple-element.30.up_own, bf16[1024,1024]{1,0:T(8,128)(2,1)S(1)} %collective-permute-done.up_other, ...), custom_call_target="tpu_custom_call" | custom-call | flops 2147483648 | bytes 4194304 | tf_op jit(solution)/shard_map/pallas_call | solution.py:41
  42.4 0.0 copy-start.1
  42.4 24.4 %all_to_all.21 = bf16[128,16,128]{2,1,0:T(8,128)(2,1)S(1)} all-to-all(bf16[128,16,128]{2,1,0:T(8,128)(2,1)S(1)} %get-tuple-element.32), channel_id=1, replica_groups=mesh['x'=4,'y_lo'=2,'z'=8,'y_hi'=2,'core'=2] {'x','y_lo','z','y_hi'}, dimensions={0} | all-to-all | bytes 1048576 | tf_op jit(solution)/shard_map/all_to_all | solution.py:28
  66.9 0.0 copy-start
  66.9 0.0 copy-start.2
  66.9 1.2 %shard_map.86 = (bf16[64,512]{1,0:T(8,128)(2,1)S(1)}, bf16[64,1024]{1,0:T(8,128)(2,1)S(1)}, bf16[512,128]{1,0:T(8,128)(2,1)S(1)}) custom-call(bf16[64,2,16,128]{3,2,1,0:T(8,128)(2,1)S(1)} %bitcast.15, bf16[512,1024]{1,0:T(8,128)(2,1)S(1)} %get-tuple-element.33.tokens, bf16[512,1024]{1,0:T(8,128)(2,1)S(1)} %get-tuple-element.34.grads, ...), custom_call_target="tpu_custom_call" | custom-call | flops 201326592 | bytes 3145728 | tf_op jit(solution)/shard_map/pallas_call | solution.py:41
  68.0 20.0 %all_to_all.22 = bf16[128,4,128]{2,1,0:T(4,128)(2,1)S(1)} all-to-all(bf16[128,4,128]{2,1,0:T(4,128)(2,1)S(1)} %bitcast.21), channel_id=1, replica_groups=mesh['x'=4,'y_lo'=2,'z'=8,'y_hi'=2,'core'=2] {'x','y_lo','z','y_hi'}, dimensions={0} | all-to-all | bytes 262144 | tf_op jit(solution)/shard_map/all_to_all | solution.py:28
  88.1 0.1 shard_map.87.a
  88.1 3.5 %collective-permute-start.2 = (f32[4,128]{1,0:T(4,128)S(1)}, f32[4,128]{1,0:T(4,128)S(1)}, u32[]{:S(2)}, u32[]{:S(2)}) collective-permute-start(f32[4,128]{1,0:T(4,128)S(1)} %shard_map.87.a), channel_id=1, source_target_pairs={{0,1},{1,0},{2,3},{3,2},{4,5},{5,4},{6,7},{7,6},{8,9},{9,8},{10,11... | collective-permute-start | bytes 6152 | tf_op jit(solution)/shard_map/ppermute | solution.py:24
  91.6 0.8 collective-permute-done.2.b
  92.4 0.0 copy-done.1
  92.4 0.3 collective-permute-start.3
  92.8 0.7 shard_map.88
  93.4 6.2 %all-to-all-start.3 = ((bf16[128,4,128]{2,1,0:T(4,128)(2,1)}), bf16[128,4,128]{2,1,0:T(4,128)(2,1)S(1)}, u32[]{:S(2)}, u32[]{:S(2)}) async-start(bf16[128,4,128]{2,1,0:T(4,128)(2,1)} %bitcast.9), calls=%async_computation.3 | async-start | bytes 262144 | tf_op jit(solution)/shard_map/all_to_all | solution.py:28
  99.6 0.0 copy-done
  99.6 1.4 %shard_map.89 = bf16[512,1024]{1,0:T(8,128)(2,1)} custom-call(f32[64,512]{1,0:T(8,128)S(1)} %get-tuple-element.35.dispatch, bf16[64,512]{1,0:T(8,128)(2,1)S(1)} %get-tuple-element.44.logit_grads, bf16[64,1024]{1,0:T(8,128)(2,1)S(1)} %get-tuple-element.45.slot_grads, bf16[64,1024]{1,0:T(8,128)(2,1)S(1)} %bitcast.17), custom_call_target="tpu_custom_call" | custom-call | flops 134217728 | bytes 2097152 | tf_op jit(solution)/shard_map/pallas_call | solution.py:41
  101.1 0.0 collective-permute-done.3.recv
  101.1 0.0 copy-done.2
  101.1 3.1 %shard_map.90 = (bf16[1024,1024]{1,0:T(8,128)(2,1)}, bf16[1024,1024]{1,0:T(8,128)(2,1)}) custom-call(bf16[2,128,1024]{2,1,0:T(8,128)(2,1)S(1)} %copy-done.2, bf16[4,128,1024]{2,1,0:T(8,128)(2,1)S(1)} %copy-done.1, bf16[4,128,1024]{2,1,0:T(8,128)(2,1)S(1)} %collective-permute-done.3.recv), custom_call_target="tpu_custom_call" | custom-call | flops 1073741824 | bytes 4194304 | tf_op jit(solution)/shard_map/pallas_call | solution.py:148
  104.2 6.7 %all-to-all-done.3 = bf16[128,4,128]{2,1,0:T(4,128)(2,1)S(1)} async-done(((bf16[128,4,128]{2,1,0:T(4,128)(2,1)}), bf16[128,4,128]{2,1,0:T(4,128)(2,1)S(1)}, u32[]{:S(2)}, u32[]{:S(2)}) %all-to-all-start.3) | async-done | bytes 131104 | tf_op jit(solution)/shard_map/all_to_all | solution.py:28
  110.9 0.7 shard_map.91
Async XLA Ops:
  0.6 37.0 %collective-permute-start = (bf16[1024,1024]{1,0:T(8,128)(2,1)}, bf16[1024,1024]{1,0:T(8,128)(2,1)S(1)}, u32[]{:S(2)}, u32[]{:S(2)}) collective-permute-start(bf16[1024,1024]{1,0:T(8,128)(2,1)} %bitcast.22), channel_id=1, source_target_pairs={{0,1},{1,0},{2,3},{3,2},{4,5},{5,4},{6,7},{7,6},{8,9},{9,8},{10,11... | collective-permute-start | bytes 6291464 | tf_op jit(solution)/shard_map/ppermute | solution.py:24
  4.0 33.7 %collective-permute-start.1 = (bf16[1024,1024]{1,0:T(8,128)(2,1)}, bf16[1024,1024]{1,0:T(8,128)(2,1)S(1)}, u32[]{:S(2)}, u32[]{:S(2)}) collective-permute-start(bf16[1024,1024]{1,0:T(8,128)(2,1)} %bitcast.24), channel_id=1, source_target_pairs={{0,1},{1,0},{2,3},{3,2},{4,5},{5,4},{6,7},{7,6},{8,9},{9,8},{10,11... | collective-permute-start | bytes 6291464 | tf_op jit(solution)/shard_map/ppermute | solution.py:24
  42.4 50.0 %copy-start.1 = (bf16[4,128,1024]{2,1,0:T(8,128)(2,1)S(1)}, bf16[4,128,1024]{2,1,0:T(8,128)(2,1)}, u32[]{:S(2)}) copy-start(bf16[4,128,1024]{2,1,0:T(8,128)(2,1)} %get-tuple-element.47.swap) | copy-start | bytes 3145732
  66.9 32.7 %copy-start = (bf16[1024,64]{0,1:T(8,128)(2,1)S(1)}, bf16[1024,64]{0,1:T(8,128)(2,1)}, u32[]{:S(2)}) copy-start(bf16[1024,64]{0,1:T(8,128)(2,1)} %param.6) | copy-start | bytes 393220
  66.9 34.2 %copy-start.2 = (bf16[2,128,1024]{2,1,0:T(8,128)(2,1)S(1)}, bf16[2,128,1024]{2,1,0:T(8,128)(2,1)}, u32[]{:S(2)}) copy-start(bf16[2,128,1024]{2,1,0:T(8,128)(2,1)} %get-tuple-element.46.keep) | copy-start | bytes 1572868
  88.1 4.3 %collective-permute-start.2 = (f32[4,128]{1,0:T(4,128)S(1)}, f32[4,128]{1,0:T(4,128)S(1)}, u32[]{:S(2)}, u32[]{:S(2)}) collective-permute-start(f32[4,128]{1,0:T(4,128)S(1)} %shard_map.87.a), channel_id=1, source_target_pairs={{0,1},{1,0},{2,3},{3,2},{4,5},{5,4},{6,7},{7,6},{8,9},{9,8},{10,11... | collective-permute-start | bytes 6152 | tf_op jit(solution)/shard_map/ppermute | solution.py:24
  92.4 8.6 %collective-permute-start.3 = (bf16[4,128,1024]{2,1,0:T(8,128)(2,1)S(1)}, bf16[4,128,1024]{2,1,0:T(8,128)(2,1)S(1)}, u32[]{:S(2)}, u32[]{:S(2)}) collective-permute-start(bf16[4,128,1024]{2,1,0:T(8,128)(2,1)S(1)} %copy-done.1), channel_id=1, source_target_pairs={{0,1},{1,0},{2,3},{3,2},{4,5},{5,4},{6,7},{7,6},{8,9},{9,8},{10,11... | collective-permute-start | bytes 3145736 | tf_op jit(solution)/shard_map/ppermute | solution.py:24
  93.4 17.5 %all-to-all-start.3 = ((bf16[128,4,128]{2,1,0:T(4,128)(2,1)}), bf16[128,4,128]{2,1,0:T(4,128)(2,1)S(1)}, u32[]{:S(2)}, u32[]{:S(2)}) async-start(bf16[128,4,128]{2,1,0:T(4,128)(2,1)} %bitcast.9), calls=%async_computation.3 | async-start | bytes 262144 | tf_op jit(solution)/shard_map/all_to_all | solution.py:28

commit v4 on v3

--- a/solution.py
+++ b/solution.py
@@ -8,9 +8,11 @@
 gelu_coeff = 0.7978845608
 cubic_coeff = 0.044715
 
-CHIPS = ("x", "y_lo", "z", "y_hi")
+CUT = {"x": 4, "y_lo": 2, "z": 8, "y_hi": 2, "core": 2}
+CHIPS = ("y_hi", "y_lo", "z", "x")
 EXPERT = ("x", "y_lo", "z")
 DP = ("y_hi", "core")
+PLANE = ("x", "y_lo", "y_hi", "core")
 F32 = jnp.float32
 BF16 = jnp.bfloat16
 LANES = 128
@@ -24,8 +26,8 @@
     return lax.ppermute(values, "core", [(0, 1), (1, 0)])
 
 
-def exchange(blocks):
-    return lax.all_to_all(blocks, CHIPS, 0, 0, tiled=True)
+def exchange(blocks, axes=CHIPS):
+    return lax.all_to_all(blocks, axes, 0, 0, tiled=True)
 
 
 def call(kernel, outs, scratch=(), flops=0, moved=0, hbm=(), hbm_outs=(), limit=4):
@@ -49,6 +51,19 @@
         )(*args)
 
     return run
+
+
+def blocks_of(slot):
+    place = {}
+    for axis in reversed(EXPERT):
+        slot, place[axis] = divmod(slot, CUT[axis])
+    found = []
+    for place["y_hi"] in range(CUT["y_hi"]):
+        block = 0
+        for axis in CHIPS:
+            block = block * CUT[axis] + place[axis]
+        found.append(block)
+    return found
 
 
 def to_blocks(scratch, values, first, rows, start=0):
@@ -88,9 +103,9 @@
     for p in range(PIECES):
         copies[1 + PIECES + p].wait()
     to_blocks(lines, dot(c.astype(BF16), grads[...], ((1,), (0,))), 8, slots)
-    blocks = lines[...].reshape(slots, 16, LANES).astype(BF16)
-    for copy in range(rows.shape[1]):
-        rows[:, copy] = blocks
+    for slot in range(slots):
+        for block in blocks_of(slot):
+            rows[block] = lines[slot * 16 : slot * 16 + 16, :].astype(BF16)
     for copy in copies[1 + 2 * PIECES :]:
         copy.wait()
 
@@ -161,10 +176,8 @@
 def back_kernel(returned, tokens, grads, dispatch, combine, logit_grads, slot_grads, blocks, lines):
     slots = logit_grads.shape[0]
     width = tokens.shape[1]
-    total = returned[:, 0].astype(F32)
-    for copy in range(1, returned.shape[1]):
-        total = total + returned[:, copy].astype(F32)
-    lines[...] = total.reshape(slots * 16, LANES)
+    for slot in range(slots):
+        lines[slot * 16 : slot * 16 + 16, :] = sum(returned[block].astype(F32) for block in blocks_of(slot))
     outputs = []
     for k in range(width // LANES):
         outputs.append(lines[pl.ds(k, slots, stride=16), :].astype(BF16))
@@ -201,16 +214,8 @@
 
 
 def sum_kernel(blocks, out):
-    rows = out.shape[0]
-    total = jnp.sum(blocks[...].astype(F32).reshape(-1, 8, LANES), axis=0)
-    out[...] = sum(total[i : i + rows] for i in range(0, 8, rows))
-
-
-def spread_kernel(a, b, out):
-    total = a[...] + b[...]
-    tile = jnp.concatenate([total] * (16 // total.shape[0]), axis=0).astype(BF16)
-    for first in range(0, out.shape[0], 16):
-        out[first : first + 16, :] = tile
+    total = jnp.sum(blocks[...].astype(F32), axis=0)
+    out[...] = jnp.broadcast_to(total.astype(out.dtype)[None], out.shape)
 
 
 def last_kernel(blocks, out):
@@ -226,14 +231,13 @@
     count, width = image_tokens.shape
     hidden = up.shape[1]
     chips = lax.axis_size(CHIPS)
-    copies = lax.axis_size("y_hi")
     slots = slot_param.shape[1]
     param = slot_param.T
     up_other = swap_cores(up)
     down_other = swap_cores(down)
     rows, dispatch, combine, image_tokens, image_grads, up_own, down_own = call(
         front_kernel,
-        [((slots, copies, 16, LANES), BF16), ((slots, count), F32), ((slots, count), F32)]
+        [((chips, 16, LANES), BF16), ((slots, count), F32), ((slots, count), F32)]
         + [((count, width), BF16)] * 2
         + [((width, hidden), BF16), ((hidden, width), BF16)],
         [
@@ -245,7 +249,7 @@
         moved=16 * width * hidden,
         hbm=(0, 1, 2, 3, 4),
     )(image_tokens, image_grads, param, up, down)
-    mine = exchange(rows.reshape(chips, 16, LANES))
+    mine = exchange(rows)
     back, keep, swap = call(
         expert_kernel,
         [((chips, 16, LANES), BF16), ((2, chips, width), BF16), ((4, chips, width), BF16)],
@@ -267,15 +271,18 @@
         [pltpu.VMEM((slots * 16, LANES), F32)],
         flops=6 * slots * count * width,
         moved=6 * count * width,
-    )(returned.reshape(slots, copies, 16, LANES), image_tokens, image_grads, dispatch, combine)
-    blocks = exchange(blocks.reshape(chips, lines // chips, LANES)).reshape(lines, LANES)
-    (block,) = call(sum_kernel, [((lines // chips, LANES), F32)])(blocks)
-    block, other, keep, swap, logit_grads, slot_grads = lax.optimization_barrier(
-        (block, swap_cores(block), keep, swap, logit_grads, slot_grads)
+    )(returned, image_tokens, image_grads, dispatch, combine)
+    plane = lax.axis_size(PLANE)
+    depth = lax.axis_size("z")
+    blocks = exchange(blocks.reshape(plane, lines // plane, LANES), PLANE)
+    (blocks,) = call(sum_kernel, [((depth, lines // plane, LANES), F32)])(blocks)
+    blocks = exchange(blocks, "z")
+    blocks, keep, swap, logit_grads, slot_grads = lax.optimization_barrier(
+        (blocks, keep, swap, logit_grads, slot_grads)
     )
     recv = swap_cores(swap)
-    (blocks,) = call(spread_kernel, [((lines, LANES), BF16)])(block, other)
-    blocks = exchange(blocks.reshape(chips, lines // chips, LANES)).reshape(lines, LANES)
+    (blocks,) = call(sum_kernel, [((plane, lines // plane, LANES), BF16)])(blocks)
+    blocks = exchange(blocks, PLANE).reshape(lines, LANES)
     grad_up, grad_down = weight_grads(keep, swap, recv)
     (grad_image,) = call(
         image_kernel,
@@ -290,8 +297,7 @@
 
 
 def solution(mesh):
-    devices = mesh.devices.reshape(4, 2, 8, 2, 2)
-    cut = Mesh(devices, ("x", "y_lo", "z", "y_hi", "core"))
+    cut = Mesh(mesh.devices.reshape(tuple(CUT.values())), tuple(CUT))
     return jax.shard_map(
         shards,
         mesh=cut,

time: 112 us -> 108 us (0.964)
  blocking collectives: 75 us -> 80.3 us
  waiting for transfers between devices: 7.54 us -> 2.94 us
  starting transfers between devices: 13.4 us -> 8.86 us
    all_to_all x3 -> x4, blocking collectives: 75 us -> 80.3 us  [exchange(): return lax.all_to_all(blocks, axes, 0, 0, tiled=True)]
    all_to_all x1, waiting for transfers between devices: 6.71 us -> 2.93 us  [exchange(): return lax.all_to_all(blocks, axes, 0, 0, tiled=True)]
    all_to_all x1, starting transfers between devices: 6.17 us -> 3.78 us  [exchange(): return lax.all_to_all(blocks, axes, 0, 0, tiled=True)]
    ppermute x4 -> x3, starting transfers between devices: 7.26 us -> 5.07 us  [swap_cores(): return lax.ppermute(values, 'core', [(0, 1), (1, 0)])]
  transfers between devices with their start and end apart: 5 -> 4, of which waited for: 2 -> 1; matrix products, arithmetic and copies ran while one was open for 0% -> 0% of each run, Pallas kernels for 7% -> 8%
where the time goes in v4:
time: 108 us
  blocking collectives  80.3 us (74%)
  Pallas kernels  14.9 us (14%)
  starting transfers between devices  8.86 us (8%)
  waiting for transfers between devices  2.94 us (3%)
    all_to_all x4, blocking collectives, exchange(): return lax.all_to_all(blocks, axes, 0, 0, tiled=True)  80.3 us
    pallas_call x7, Pallas kernels, run(): pl.pallas_call(kernel, out_shape=[shape_of(i, shape, dtype) for i, (shape...  11.8 us
    ppermute x3, starting transfers between devices, swap_cores(): return lax.ppermute(values, 'core', [(0, 1), (1, 0)])  5.07 us
    all_to_all x1, starting transfers between devices, exchange(): return lax.all_to_all(blocks, axes, 0, 0, tiled=True)  3.78 us
    pallas_call x1, Pallas kernels, weight_grads(): pl.pallas_call(weights_kernel, grid=(width // step,), out_shape=[jax.Shap...  3.11 us
    all_to_all x1, waiting for transfers between devices, exchange(): return lax.all_to_all(blocks, axes, 0, 0, tiled=True)  2.93 us
  transfers between devices with their start and end apart: 4, of which 1 were waited for; matrix products, arithmetic and copies ran while one was open for 0% of the time, Pallas kernels for 8%

profile of v4, /device:TPU:1, one launch (start us, length us, event | category | flops | bytes accessed | tf_op | source)
XLA Modules:
  0.0 107.7 jit_solution(4569606926182848783)
XLA Ops:
  0.6 3.3 %collective-permute-start = (bf16[1024,1024]{1,0:T(8,128)(2,1)}, bf16[1024,1024]{1,0:T(8,128)(2,1)S(1)}, u32[]{:S(2)}, u32[]{:S(2)}) collective-permute-start(bf16[1024,1024]{1,0:T(8,128)(2,1)} %bitcast.15), channel_id=1, source_target_pairs={{0,1},{1,0},{2,3},{3,2},{4,5},{5,4},{6,7},{7,6},{8,9},{9,8},{10,11... | collective-permute-start | bytes 6291464 | tf_op jit(solution)/shard_map/ppermute | solution.py:26
  4.0 0.1 collective-permute-start.1
  4.1 3.0 %shard_map.84 = (bf16[128,16,128]{2,1,0:T(8,128)(2,1)S(1)}, f32[64,512]{1,0:T(8,128)S(1)}, f32[64,512]{1,0:T(8,128)S(1)}, bf16[512,1024]{1,0:T(8,128)(2,1)S(1)},...) custom-call(bf16[512,1024]{1,0:T(8,128)(2,1)} %bitcast.19, ...), custom_call_target="tpu_custom_call" | custom-call | flops 201326592 | bytes 16777216 | tf_op jit(solution)/shard_map/pallas_call | solution.py:43
  7.1 30.7 %all_to_all.25.mine = bf16[128,16,128]{2,1,0:T(8,128)(2,1)S(1)} all-to-all(bf16[128,16,128]{2,1,0:T(8,128)(2,1)S(1)} %get-tuple-element.28), channel_id=1, replica_groups=mesh['x'=4,'y_lo'=2,'z'=8,'y_hi'=2,'core'=2] {'y_hi','y_lo','z','x'}, dimensions={0} | all-to-all | bytes 1048576 | tf_op jit(solution)/shard_map/all_to_all | solution.py:30
  37.8 0.0 collective-permute-done.up_other
  37.8 0.0 collective-permute-done.1.down_other
  37.8 4.8 %shard_map.85 = (bf16[128,16,128]{2,1,0:T(8,128)(2,1)S(1)}, bf16[2,128,1024]{2,1,0:T(8,128)(2,1)}, bf16[4,128,1024]{2,1,0:T(8,128)(2,1)}) custom-call(bf16[128,16,128]{2,1,0:T(8,128)(2,1)S(1)} %all_to_all.25.mine, bf16[1024,1024]{1,0:T(8,128)(2,1)S(1)} %get-tuple-element.29.up_own, bf16[1024,1024]{1,0:T(8,128)(2,1)S(1)} %collective-permute-done.up_other, ...), custom_call_target="tpu_custom_call" | custom-call | flops 2147483648 | bytes 4194304 | tf_op jit(solution)/shard_map/pallas_call | solution.py:43
  42.6 0.0 copy-start.1
  42.6 24.1 %all_to_all.26.returned = bf16[128,16,128]{2,1,0:T(8,128)(2,1)S(1)} all-to-all(bf16[128,16,128]{2,1,0:T(8,128)(2,1)S(1)} %get-tuple-element.31), channel_id=1, replica_groups=mesh['x'=4,'y_lo'=2,'z'=8,'y_hi'=2,'core'=2] {'y_hi','y_lo','z','x'}, dimensions={0} | all-to-all | bytes 1048576 | tf_op jit(solution)/shard_map/all_to_all | solution.py:30
  66.7 0.0 copy-start
  66.7 0.0 copy-start.2
  66.7 1.1 %shard_map.86 = (bf16[64,512]{1,0:T(8,128)(2,1)S(1)}, bf16[64,1024]{1,0:T(8,128)(2,1)S(1)}, bf16[512,128]{1,0:T(8,128)(2,1)S(1)}) custom-call(bf16[128,16,128]{2,1,0:T(8,128)(2,1)S(1)} %all_to_all.26.returned, bf16[512,1024]{1,0:T(8,128)(2,1)S(1)} %get-tuple-element.32.tokens, bf16[512,1024]{1,0:T(8,128)(2,1)S(1)} %get-tuple-element.33.grads, ...), custom_call_target="tpu_custom_call" | custom-call | flops 201326592 | bytes 3145728 | tf_op jit(solution)/shard_map/pallas_call | solution.py:43
  67.9 15.9 %all_to_all.27.blocks = bf16[32,16,128]{2,1,0:T(8,128)(2,1)S(1)} all-to-all(bf16[32,16,128]{2,1,0:T(8,128)(2,1)S(1)} %bitcast.14), channel_id=1, replica_groups=mesh['x'=4,'y_lo'=2,'z'=8,'y_hi'=2,'core'=2] {'x','y_lo','y_hi','core'}, dimensions={0} | all-to-all | bytes 262144 | tf_op jit(solution)/shard_map/all_to_all | solution.py:30
  83.9 9.6 %all_to_all.28.blocks = f32[8,16,128]{2,1,0:T(8,128)S(1)} all-to-all(f32[8,16,128]{2,1,0:T(8,128)S(1)} %shard_map.87), channel_id=1, replica_groups=mesh['x'=4,'y_lo'=2,'z'=8,'y_hi'=2,'core'=2] {'z'}, dimensions={0} | all-to-all | bytes 131072 | tf_op jit(solution)/shard_map/all_to_all | solution.py:30
  93.4 0.0 copy-done.1
  93.4 1.6 %collective-permute-start.2 = (bf16[4,128,1024]{2,1,0:T(8,128)(2,1)S(1)}, bf16[4,128,1024]{2,1,0:T(8,128)(2,1)S(1)}, u32[]{:S(2)}, u32[]{:S(2)}) collective-permute-start(bf16[4,128,1024]{2,1,0:T(8,128)(2,1)S(1)} %copy-done.1), channel_id=1, source_target_pairs={{0,1},{1,0},{2,3},{3,2},{4,5},{5,4},{6,7},{7,6},{8,9},{9,8},{10,11... | collective-permute-start | bytes 3145736 | tf_op jit(solution)/shard_map/ppermute | solution.py:26
  95.1 0.7 shard_map.88
  95.7 3.8 %all-to-all-start.4 = ((bf16[32,16,128]{2,1,0:T(8,128)(2,1)}), bf16[32,16,128]{2,1,0:T(8,128)(2,1)S(1)}, u32[]{:S(2)}, u32[]{:S(2)}) async-start(bf16[32,16,128]{2,1,0:T(8,128)(2,1)} %shard_map.88), calls=%async_computation.4 | async-start | bytes 262144 | tf_op jit(solution)/shard_map/all_to_all | solution.py:30
  99.5 0.0 copy-done
  99.5 1.4 %shard_map.89 = bf16[512,1024]{1,0:T(8,128)(2,1)} custom-call(f32[64,512]{1,0:T(8,128)S(1)} %get-tuple-element.34.dispatch, bf16[64,512]{1,0:T(8,128)(2,1)S(1)} %get-tuple-element.42.logit_grads, bf16[64,1024]{1,0:T(8,128)(2,1)S(1)} %get-tuple-element.43.slot_grads, bf16[64,1024]{1,0:T(8,128)(2,1)S(1)} %bitcast.12), custom_call_target="tpu_custom_call" | custom-call | flops 134217728 | bytes 2097152 | tf_op jit(solution)/shard_map/pallas_call | solution.py:43
  101.0 0.0 collective-permute-done.2.recv
  101.0 0.0 copy-done.2
  101.0 3.1 %shard_map.90 = (bf16[1024,1024]{1,0:T(8,128)(2,1)}, bf16[1024,1024]{1,0:T(8,128)(2,1)}) custom-call(bf16[2,128,1024]{2,1,0:T(8,128)(2,1)S(1)} %copy-done.2, bf16[4,128,1024]{2,1,0:T(8,128)(2,1)S(1)} %copy-done.1, bf16[4,128,1024]{2,1,0:T(8,128)(2,1)S(1)} %collective-permute-done.2.recv), custom_call_target="tpu_custom_call" | custom-call | flops 1073741824 | bytes 4194304 | tf_op jit(solution)/shard_map/pallas_call | solution.py:163
  104.1 2.9 %all-to-all-done.4 = bf16[32,16,128]{2,1,0:T(8,128)(2,1)S(1)} async-done(((bf16[32,16,128]{2,1,0:T(8,128)(2,1)}), bf16[32,16,128]{2,1,0:T(8,128)(2,1)S(1)}, u32[]{:S(2)}, u32[]{:S(2)}) %all-to-all-start.4) | async-done | bytes 131104 | tf_op jit(solution)/shard_map/all_to_all | solution.py:30
  107.0 0.7 shard_map.91
  (1 shorter events, 0.0 us)
Async XLA Ops:
  0.6 37.2 %collective-permute-start = (bf16[1024,1024]{1,0:T(8,128)(2,1)}, bf16[1024,1024]{1,0:T(8,128)(2,1)S(1)}, u32[]{:S(2)}, u32[]{:S(2)}) collective-permute-start(bf16[1024,1024]{1,0:T(8,128)(2,1)} %bitcast.15), channel_id=1, source_target_pairs={{0,1},{1,0},{2,3},{3,2},{4,5},{5,4},{6,7},{7,6},{8,9},{9,8},{10,11... | collective-permute-start | bytes 6291464 | tf_op jit(solution)/shard_map/ppermute | solution.py:26
  4.0 33.9 %collective-permute-start.1 = (bf16[1024,1024]{1,0:T(8,128)(2,1)}, bf16[1024,1024]{1,0:T(8,128)(2,1)S(1)}, u32[]{:S(2)}, u32[]{:S(2)}) collective-permute-start(bf16[1024,1024]{1,0:T(8,128)(2,1)} %bitcast.17), channel_id=1, source_target_pairs={{0,1},{1,0},{2,3},{3,2},{4,5},{5,4},{6,7},{7,6},{8,9},{9,8},{10,11... | collective-permute-start | bytes 6291464 | tf_op jit(solution)/shard_map/ppermute | solution.py:26
  42.6 50.8 %copy-start.1 = (bf16[4,128,1024]{2,1,0:T(8,128)(2,1)S(1)}, bf16[4,128,1024]{2,1,0:T(8,128)(2,1)}, u32[]{:S(2)}) copy-start(bf16[4,128,1024]{2,1,0:T(8,128)(2,1)} %get-tuple-element.45.swap) | copy-start | bytes 3145732
  66.7 32.8 %copy-start = (bf16[1024,64]{0,1:T(8,128)(2,1)S(1)}, bf16[1024,64]{0,1:T(8,128)(2,1)}, u32[]{:S(2)}) copy-start(bf16[1024,64]{0,1:T(8,128)(2,1)} %param.6) | copy-start | bytes 393220
  66.7 34.2 %copy-start.2 = (bf16[2,128,1024]{2,1,0:T(8,128)(2,1)S(1)}, bf16[2,128,1024]{2,1,0:T(8,128)(2,1)}, u32[]{:S(2)}) copy-start(bf16[2,128,1024]{2,1,0:T(8,128)(2,1)} %get-tuple-element.44.keep) | copy-start | bytes 1572868
  93.4 7.5 %collective-permute-start.2 = (bf16[4,128,1024]{2,1,0:T(8,128)(2,1)S(1)}, bf16[4,128,1024]{2,1,0:T(8,128)(2,1)S(1)}, u32[]{:S(2)}, u32[]{:S(2)}) collective-permute-start(bf16[4,128,1024]{2,1,0:T(8,128)(2,1)S(1)} %copy-done.1), channel_id=1, source_target_pairs={{0,1},{1,0},{2,3},{3,2},{4,5},{5,4},{6,7},{7,6},{8,9},{9,8},{10,11... | collective-permute-start | bytes 3145736 | tf_op jit(solution)/shard_map/ppermute | solution.py:26
  95.7 11.3 %all-to-all-start.4 = ((bf16[32,16,128]{2,1,0:T(8,128)(2,1)}), bf16[32,16,128]{2,1,0:T(8,128)(2,1)S(1)}, u32[]{:S(2)}, u32[]{:S(2)}) async-start(bf16[32,16,128]{2,1,0:T(8,128)(2,1)} %shard_map.88), calls=%async_computation.4 | async-start | bytes 262144 | tf_op jit(solution)/shard_map/all_to_all | solution.py:30

commit v5 on v4

--- a/solution.py
+++ b/solution.py
@@ -88,11 +88,9 @@
     for copy in copies:
         copy.start()
     copies[0].wait()
-    logits = []
     for p in range(PIECES):
         copies[1 + p].wait()
-        logits.append(dot(param[...], tokens[p * piece : (p + 1) * piece, :], ((1,), (1,))))
-    logits = jnp.concatenate(logits, axis=1)
+    logits = dot(param[...], tokens[...], ((1,), (1,)))
     e = jnp.exp(logits - jnp.max(logits, axis=1, keepdims=True))
     d = e / jnp.sum(e, axis=1, keepdims=True)
     e = jnp.exp(logits - jnp.max(logits, axis=0, keepdims=True))
@@ -116,10 +114,10 @@
     blocks = mine[...]
     parts[0] = blocks[:, :8].reshape(images, width)
     parts[1] = blocks[:, 8:].reshape(images, width)
-    targets = [swap.at[j] for j in range(4)] + [keep.at[j] for j in range(2)]
-    copies = [pltpu.make_async_copy(parts.at[j], targets[j], sems.at[j]) for j in range(6)]
-    copies[0].start()
-    copies[1].start()
+    copies = [
+        pltpu.make_async_copy(parts.at[pl.ds(0, 4)], swap, sems.at[0]),
+        pltpu.make_async_copy(parts.at[pl.ds(4, 2)], keep, sems.at[1]),
+    ]
     rows_in = parts[0]
     rows_grad = parts[1]
     for up, down, first in ((up_other, down_other, 2), (up_own, down_own, 4)):
@@ -133,15 +131,14 @@
             )
             g = dot(rows_grad, down[cols, :], ((1,), (1,)))
             parts[first + 1, :, cols] = (g * slope).astype(BF16)
-        copies[first].start()
-        copies[first + 1].start()
+        copies[first // 2 - 1].start()
     for n in range(0, width, 256):
         cols = slice(n, n + 256)
         out = dot(parts[4], down_own[:, cols], ((1,), (0,))) + dot(parts[2], down_other[:, cols], ((1,), (0,)))
         to_blocks(lines, out, n // LANES, images)
         out = dot(parts[5], up_own[cols, :], ((1,), (1,))) + dot(parts[3], up_other[cols, :], ((1,), (1,)))
         to_blocks(lines, out, 8 + n // LANES, images)
-    back[...] = lines[...].reshape(images, 16, LANES).astype(BF16)
+    back[...] = lines[: images * 16, :].reshape(images, 16, LANES).astype(BF16)
     for copy in copies:
         copy.wait()
 
@@ -242,7 +239,7 @@
         + [((width, hidden), BF16), ((hidden, width), BF16)],
         [
             pltpu.VMEM((slots, width), BF16),
-            pltpu.VMEM((slots * 16, LANES), F32),
+            pltpu.VMEM((slots * 16 + 16, LANES), F32),
             pltpu.SemaphoreType.DMA((2 * PIECES + 3,)),
         ],
         flops=6 * slots * count * width,
@@ -255,8 +252,8 @@
         [((chips, 16, LANES), BF16), ((2, chips, width), BF16), ((4, chips, width), BF16)],
         [
             pltpu.VMEM((6, chips, width), BF16),
-            pltpu.VMEM((chips * 16, LANES), F32),
-            pltpu.SemaphoreType.DMA((6,)),
+            pltpu.VMEM((chips * 16 + 16, LANES), F32),
+            pltpu.SemaphoreType.DMA((2,)),
         ],
         flops=16 * chips * width * hidden,
         moved=4 * width * hidden,
@@ -268,7 +265,7 @@
     logit_grads, slot_grads, blocks = call(
         back_kernel,
         [((slots, count), BF16), ((slots, width), BF16), ((lines, LANES), BF16)],
-        [pltpu.VMEM((slots * 16, LANES), F32)],
+        [pltpu.VMEM((slots * 16 + 16, LANES), F32)],
         flops=6 * slots * count * width,
         moved=6 * count * width,
     )(returned, image_tokens, image_grads, dispatch, combine)

time: 108 us -> 108 us (level)
  no operation moved by 1% of the time
where the time goes in v5:
time: 108 us
  blocking collectives  80.3 us (74%)
  Pallas kernels  14.9 us (14%)
  starting transfers between devices  8.86 us (8%)
  waiting for transfers between devices  2.9 us (3%)
    all_to_all x4, blocking collectives, exchange(): return lax.all_to_all(blocks, axes, 0, 0, tiled=True)  80.3 us
    pallas_call x7, Pallas kernels, run(): pl.pallas_call(kernel, out_shape=[shape_of(i, shape, dtype) for i, (shape...  11.8 us
    ppermute x3, starting transfers between devices, swap_cores(): return lax.ppermute(values, 'core', [(0, 1), (1, 0)])  5.07 us
    all_to_all x1, starting transfers between devices, exchange(): return lax.all_to_all(blocks, axes, 0, 0, tiled=True)  3.78 us
    pallas_call x1, Pallas kernels, weight_grads(): pl.pallas_call(weights_kernel, grid=(width // step,), out_shape=[jax.Shap...  3.15 us
    all_to_all x1, waiting for transfers between devices, exchange(): return lax.all_to_all(blocks, axes, 0, 0, tiled=True)  2.89 us
  transfers between devices with their start and end apart: 4, of which 1 were waited for; matrix products, arithmetic and copies ran while one was open for 0% of the time, Pallas kernels for 8%

profile of v5, /device:TPU:1, one launch (start us, length us, event | category | flops | bytes accessed | tf_op | source)
XLA Modules:
  0.0 107.7 jit_solution(13012275927723976153)
XLA Ops:
  0.6 3.3 %collective-permute-start = (bf16[1024,1024]{1,0:T(8,128)(2,1)}, bf16[1024,1024]{1,0:T(8,128)(2,1)S(1)}, u32[]{:S(2)}, u32[]{:S(2)}) collective-permute-start(bf16[1024,1024]{1,0:T(8,128)(2,1)} %bitcast.15), channel_id=1, source_target_pairs={{0,1},{1,0},{2,3},{3,2},{4,5},{5,4},{6,7},{7,6},{8,9},{9,8},{10,11... | collective-permute-start | bytes 6291464 | tf_op jit(solution)/shard_map/ppermute | solution.py:26
  4.0 0.1 collective-permute-start.1
  4.1 3.0 %shard_map.84 = (bf16[128,16,128]{2,1,0:T(8,128)(2,1)S(1)}, f32[64,512]{1,0:T(8,128)S(1)}, f32[64,512]{1,0:T(8,128)S(1)}, bf16[512,1024]{1,0:T(8,128)(2,1)S(1)},...) custom-call(bf16[512,1024]{1,0:T(8,128)(2,1)} %bitcast.19, ...), custom_call_target="tpu_custom_call" | custom-call | flops 201326592 | bytes 16777216 | tf_op jit(solution)/shard_map/pallas_call | solution.py:43
  7.1 30.7 %all_to_all.25.mine = bf16[128,16,128]{2,1,0:T(8,128)(2,1)S(1)} all-to-all(bf16[128,16,128]{2,1,0:T(8,128)(2,1)S(1)} %get-tuple-element.28), channel_id=1, replica_groups=mesh['x'=4,'y_lo'=2,'z'=8,'y_hi'=2,'core'=2] {'y_hi','y_lo','z','x'}, dimensions={0} | all-to-all | bytes 1048576 | tf_op jit(solution)/shard_map/all_to_all | solution.py:30
  37.8 0.0 collective-permute-done.up_other
  37.8 0.0 collective-permute-done.1.down_other
  37.8 4.7 %shard_map.85 = (bf16[128,16,128]{2,1,0:T(8,128)(2,1)S(1)}, bf16[2,128,1024]{2,1,0:T(8,128)(2,1)}, bf16[4,128,1024]{2,1,0:T(8,128)(2,1)}) custom-call(bf16[128,16,128]{2,1,0:T(8,128)(2,1)S(1)} %all_to_all.25.mine, bf16[1024,1024]{1,0:T(8,128)(2,1)S(1)} %get-tuple-element.29.up_own, bf16[1024,1024]{1,0:T(8,128)(2,1)S(1)} %collective-permute-done.up_other, ...), custom_call_target="tpu_custom_call" | custom-call | flops 2147483648 | bytes 4194304 | tf_op jit(solution)/shard_map/pallas_call | solution.py:43
  42.6 0.0 copy-start.1
  42.6 24.1 %all_to_all.26.returned = bf16[128,16,128]{2,1,0:T(8,128)(2,1)S(1)} all-to-all(bf16[128,16,128]{2,1,0:T(8,128)(2,1)S(1)} %get-tuple-element.31), channel_id=1, replica_groups=mesh['x'=4,'y_lo'=2,'z'=8,'y_hi'=2,'core'=2] {'y_hi','y_lo','z','x'}, dimensions={0} | all-to-all | bytes 1048576 | tf_op jit(solution)/shard_map/all_to_all | solution.py:30
  66.7 0.0 copy-start
  66.7 0.0 copy-start.2
  66.7 1.1 %shard_map.86 = (bf16[64,512]{1,0:T(8,128)(2,1)S(1)}, bf16[64,1024]{1,0:T(8,128)(2,1)S(1)}, bf16[512,128]{1,0:T(8,128)(2,1)S(1)}) custom-call(bf16[128,16,128]{2,1,0:T(8,128)(2,1)S(1)} %all_to_all.26.returned, bf16[512,1024]{1,0:T(8,128)(2,1)S(1)} %get-tuple-element.32.tokens, bf16[512,1024]{1,0:T(8,128)(2,1)S(1)} %get-tuple-element.33.grads, ...), custom_call_target="tpu_custom_call" | custom-call | flops 201326592 | bytes 3145728 | tf_op jit(solution)/shard_map/pallas_call | solution.py:43
  67.8 15.9 %all_to_all.27.blocks = bf16[32,16,128]{2,1,0:T(8,128)(2,1)S(1)} all-to-all(bf16[32,16,128]{2,1,0:T(8,128)(2,1)S(1)} %bitcast.14), channel_id=1, replica_groups=mesh['x'=4,'y_lo'=2,'z'=8,'y_hi'=2,'core'=2] {'x','y_lo','y_hi','core'}, dimensions={0} | all-to-all | bytes 262144 | tf_op jit(solution)/shard_map/all_to_all | solution.py:30
  83.8 9.6 %all_to_all.28.blocks = f32[8,16,128]{2,1,0:T(8,128)S(1)} all-to-all(f32[8,16,128]{2,1,0:T(8,128)S(1)} %shard_map.87), channel_id=1, replica_groups=mesh['x'=4,'y_lo'=2,'z'=8,'y_hi'=2,'core'=2] {'z'}, dimensions={0} | all-to-all | bytes 131072 | tf_op jit(solution)/shard_map/all_to_all | solution.py:30
  93.4 0.0 copy-done.1
  93.4 1.6 %collective-permute-start.2 = (bf16[4,128,1024]{2,1,0:T(8,128)(2,1)S(1)}, bf16[4,128,1024]{2,1,0:T(8,128)(2,1)S(1)}, u32[]{:S(2)}, u32[]{:S(2)}) collective-permute-start(bf16[4,128,1024]{2,1,0:T(8,128)(2,1)S(1)} %copy-done.1), channel_id=1, source_target_pairs={{0,1},{1,0},{2,3},{3,2},{4,5},{5,4},{6,7},{7,6},{8,9},{9,8},{10,11... | collective-permute-start | bytes 3145736 | tf_op jit(solution)/shard_map/ppermute | solution.py:26
  95.0 0.7 shard_map.88
  95.7 3.8 %all-to-all-start.4 = ((bf16[32,16,128]{2,1,0:T(8,128)(2,1)}), bf16[32,16,128]{2,1,0:T(8,128)(2,1)S(1)}, u32[]{:S(2)}, u32[]{:S(2)}) async-start(bf16[32,16,128]{2,1,0:T(8,128)(2,1)} %shard_map.88), calls=%async_computation.4 | async-start | bytes 262144 | tf_op jit(solution)/shard_map/all_to_all | solution.py:30
  99.5 0.0 copy-done
  99.5 1.4 %shard_map.89 = bf16[512,1024]{1,0:T(8,128)(2,1)} custom-call(f32[64,512]{1,0:T(8,128)S(1)} %get-tuple-element.34.dispatch, bf16[64,512]{1,0:T(8,128)(2,1)S(1)} %get-tuple-element.42.logit_grads, bf16[64,1024]{1,0:T(8,128)(2,1)S(1)} %get-tuple-element.43.slot_grads, bf16[64,1024]{1,0:T(8,128)(2,1)S(1)} %bitcast.12), custom_call_target="tpu_custom_call" | custom-call | flops 134217728 | bytes 2097152 | tf_op jit(solution)/shard_map/pallas_call | solution.py:43
  100.9 0.0 collective-permute-done.2.recv
  100.9 0.0 copy-done.2
  100.9 3.2 %shard_map.90 = (bf16[1024,1024]{1,0:T(8,128)(2,1)}, bf16[1024,1024]{1,0:T(8,128)(2,1)}) custom-call(bf16[2,128,1024]{2,1,0:T(8,128)(2,1)S(1)} %copy-done.2, bf16[4,128,1024]{2,1,0:T(8,128)(2,1)S(1)} %copy-done.1, bf16[4,128,1024]{2,1,0:T(8,128)(2,1)S(1)} %collective-permute-done.2.recv), custom_call_target="tpu_custom_call" | custom-call | flops 1073741824 | bytes 4194304 | tf_op jit(solution)/shard_map/pallas_call | solution.py:160
  104.1 2.9 %all-to-all-done.4 = bf16[32,16,128]{2,1,0:T(8,128)(2,1)S(1)} async-done(((bf16[32,16,128]{2,1,0:T(8,128)(2,1)}), bf16[32,16,128]{2,1,0:T(8,128)(2,1)S(1)}, u32[]{:S(2)}, u32[]{:S(2)}) %all-to-all-start.4) | async-done | bytes 131104 | tf_op jit(solution)/shard_map/all_to_all | solution.py:30
  107.0 0.7 shard_map.91
  (1 shorter events, 0.0 us)
Async XLA Ops:
  0.6 37.2 %collective-permute-start = (bf16[1024,1024]{1,0:T(8,128)(2,1)}, bf16[1024,1024]{1,0:T(8,128)(2,1)S(1)}, u32[]{:S(2)}, u32[]{:S(2)}) collective-permute-start(bf16[1024,1024]{1,0:T(8,128)(2,1)} %bitcast.15), channel_id=1, source_target_pairs={{0,1},{1,0},{2,3},{3,2},{4,5},{5,4},{6,7},{7,6},{8,9},{9,8},{10,11... | collective-permute-start | bytes 6291464 | tf_op jit(solution)/shard_map/ppermute | solution.py:26
  4.0 33.9 %collective-permute-start.1 = (bf16[1024,1024]{1,0:T(8,128)(2,1)}, bf16[1024,1024]{1,0:T(8,128)(2,1)S(1)}, u32[]{:S(2)}, u32[]{:S(2)}) collective-permute-start(bf16[1024,1024]{1,0:T(8,128)(2,1)} %bitcast.17), channel_id=1, source_target_pairs={{0,1},{1,0},{2,3},{3,2},{4,5},{5,4},{6,7},{7,6},{8,9},{9,8},{10,11... | collective-permute-start | bytes 6291464 | tf_op jit(solution)/shard_map/ppermute | solution.py:26
  42.6 50.8 %copy-start.1 = (bf16[4,128,1024]{2,1,0:T(8,128)(2,1)S(1)}, bf16[4,128,1024]{2,1,0:T(8,128)(2,1)}, u32[]{:S(2)}) copy-start(bf16[4,128,1024]{2,1,0:T(8,128)(2,1)} %get-tuple-element.45.swap) | copy-start | bytes 3145732
  66.7 32.8 %copy-start = (bf16[1024,64]{0,1:T(8,128)(2,1)S(1)}, bf16[1024,64]{0,1:T(8,128)(2,1)}, u32[]{:S(2)}) copy-start(bf16[1024,64]{0,1:T(8,128)(2,1)} %param.6) | copy-start | bytes 393220
  66.7 34.2 %copy-start.2 = (bf16[2,128,1024]{2,1,0:T(8,128)(2,1)S(1)}, bf16[2,128,1024]{2,1,0:T(8,128)(2,1)}, u32[]{:S(2)}) copy-start(bf16[2,128,1024]{2,1,0:T(8,128)(2,1)} %get-tuple-element.44.keep) | copy-start | bytes 1572868
  93.4 7.6 %collective-permute-start.2 = (bf16[4,128,1024]{2,1,0:T(8,128)(2,1)S(1)}, bf16[4,128,1024]{2,1,0:T(8,128)(2,1)S(1)}, u32[]{:S(2)}, u32[]{:S(2)}) collective-permute-start(bf16[4,128,1024]{2,1,0:T(8,128)(2,1)S(1)} %copy-done.1), channel_id=1, source_target_pairs={{0,1},{1,0},{2,3},{3,2},{4,5},{5,4},{6,7},{7,6},{8,9},{9,8},{10,11... | collective-permute-start | bytes 3145736 | tf_op jit(solution)/shard_map/ppermute | solution.py:26
  95.7 11.3 %all-to-all-start.4 = ((bf16[32,16,128]{2,1,0:T(8,128)(2,1)}), bf16[32,16,128]{2,1,0:T(8,128)(2,1)S(1)}, u32[]{:S(2)}, u32[]{:S(2)}) async-start(bf16[32,16,128]{2,1,0:T(8,128)(2,1)} %shard_map.88), calls=%async_computation.4 | async-start | bytes 262144 | tf_op jit(solution)/shard_map/all_to_all | solution.py:30

commit v6 on v5

--- a/solution.py
+++ b/solution.py
@@ -1,5 +1,8 @@
+import math
+
 import jax
 import jax.numpy as jnp
+import numpy as np
 from jax import lax
 from jax.experimental import pallas as pl
 from jax.experimental.pallas import tpu as pltpu
@@ -10,6 +13,7 @@
 
 CUT = {"x": 4, "y_lo": 2, "z": 8, "y_hi": 2, "core": 2}
 CHIPS = ("y_hi", "y_lo", "z", "x")
+ROOT = {"x": 2, "y_lo": 0, "z": 6, "y_hi": 1}
 EXPERT = ("x", "y_lo", "z")
 DP = ("y_hi", "core")
 PLANE = ("x", "y_lo", "y_hi", "core")
@@ -26,8 +30,14 @@
     return lax.ppermute(values, "core", [(0, 1), (1, 0)])
 
 
-def exchange(blocks, axes=CHIPS):
-    return lax.all_to_all(blocks, axes, 0, 0, tiled=True)
+def exchange(blocks, axes):
+    numbers = np.arange(math.prod(CUT.values())).reshape(tuple(CUT.values()))
+    for axis, first in ROOT.items():
+        numbers = np.roll(numbers, -first, axis=list(CUT).index(axis))
+    order = [axis for axis in CUT if axis not in axes] + list(axes)
+    numbers = numbers.transpose([list(CUT).index(axis) for axis in order])
+    groups = numbers.reshape(-1, math.prod(CUT[axis] for axis in axes)).tolist()
+    return lax.all_to_all(blocks, tuple(CUT), 0, 0, axis_index_groups=groups, tiled=True)
 
 
 def call(kernel, outs, scratch=(), flops=0, moved=0, hbm=(), hbm_outs=(), limit=4):
@@ -61,7 +71,7 @@
     for place["y_hi"] in range(CUT["y_hi"]):
         block = 0
         for axis in CHIPS:
-            block = block * CUT[axis] + place[axis]
+            block = block * CUT[axis] + (place[axis] - ROOT[axis]) % CUT[axis]
         found.append(block)
     return found
 
@@ -246,7 +256,7 @@
         moved=16 * width * hidden,
         hbm=(0, 1, 2, 3, 4),
     )(image_tokens, image_grads, param, up, down)
-    mine = exchange(rows)
+    mine = exchange(rows, CHIPS)
     back, keep, swap = call(
         expert_kernel,
         [((chips, 16, LANES), BF16), ((2, chips, width), BF16), ((4, chips, width), BF16)],
@@ -260,7 +270,7 @@
         hbm_outs=(1, 2),
         limit=8,
     )(mine, up_own, up_other, down_own, down_other)
-    returned = exchange(back)
+    returned = exchange(back, CHIPS)
     lines = slots * width // LANES
     logit_grads, slot_grads, blocks = call(
         back_kernel,
@@ -273,7 +283,7 @@
     depth = lax.axis_size("z")
     blocks = exchange(blocks.reshape(plane, lines // plane, LANES), PLANE)
     (blocks,) = call(sum_kernel, [((depth, lines // plane, LANES), F32)])(blocks)
-    blocks = exchange(blocks, "z")
+    blocks = exchange(blocks, ("z",))
     blocks, keep, swap, logit_grads, slot_grads = lax.optimization_barrier(
         (blocks, keep, swap, logit_grads, slot_grads)
     )

time: 108 us -> 103 us (0.954)
  blocking collectives: 80.3 us -> 74.5 us
  starting transfers between devices: 8.86 us -> 12.7 us
  waiting for transfers between devices: 2.9 us -> 0.01 us
    all_to_all x4, blocking collectives: 80.3 us -> 74.5 us  [exchange(): lax.all_to_all(blocks, tuple(CUT), 0, 0, axis_index_groups=groups, tiled=...]
    all_to_all x1, starting transfers between devices: 3.78 us -> 8.16 us  [exchange(): lax.all_to_all(blocks, tuple(CUT), 0, 0, axis_index_groups=groups, tiled=...]
    all_to_all x1, waiting for transfers between devices: 2.89 us -> 0.01 us  [exchange(): lax.all_to_all(blocks, tuple(CUT), 0, 0, axis_index_groups=groups, tiled=...]
  transfers between devices with their start and end apart: 4 -> 4, of which waited for: 1 -> 0; matrix products, arithmetic and copies ran while one was open for 0% -> 0% of each run, Pallas kernels for 8% -> 8%
where the time goes in v6:
time: 103 us
  blocking collectives  74.5 us (72%)
  Pallas kernels  14.9 us (14%)
  starting transfers between devices  12.7 us (12%)
    all_to_all x4, blocking collectives, exchange(): lax.all_to_all(blocks, tuple(CUT), 0, 0, axis_index_groups=groups, tiled=...  74.5 us
    pallas_call x7, Pallas kernels, run(): pl.pallas_call(kernel, out_shape=[shape_of(i, shape, dtype) for i, (shape...  11.8 us
    all_to_all x1, starting transfers between devices, exchange(): lax.all_to_all(blocks, tuple(CUT), 0, 0, axis_index_groups=groups, tiled=...  8.16 us
    ppermute x3, starting transfers between devices, swap_cores(): return lax.ppermute(values, 'core', [(0, 1), (1, 0)])  4.55 us
    pallas_call x1, Pallas kernels, weight_grads(): pl.pallas_call(weights_kernel, grid=(width // step,), out_shape=[jax.Shap...  3.13 us
  transfers between devices with their start and end apart: 4, of which 0 were waited for; matrix products, arithmetic and copies ran while one was open for 0% of the time, Pallas kernels for 8%

profile of v6, /device:TPU:1, one launch (start us, length us, event | category | flops | bytes accessed | tf_op | source)
XLA Modules:
  0.0 102.8 jit_solution(13934523593607972974)
XLA Ops:
  0.6 3.3 %collective-permute-start = (bf16[1024,1024]{1,0:T(8,128)(2,1)}, bf16[1024,1024]{1,0:T(8,128)(2,1)S(1)}, u32[]{:S(2)}, u32[]{:S(2)}) collective-permute-start(bf16[1024,1024]{1,0:T(8,128)(2,1)} %bitcast.15), channel_id=1, source_target_pairs={{0,1},{1,0},{2,3},{3,2},{4,5},{5,4},{6,7},{7,6},{8,9},{9,8},{10,11... | collective-permute-start | bytes 6291464 | tf_op jit(solution)/shard_map/ppermute | solution.py:30
  4.0 0.1 collective-permute-start.1
  4.1 3.0 %shard_map.84 = (bf16[128,16,128]{2,1,0:T(8,128)(2,1)S(1)}, f32[64,512]{1,0:T(8,128)S(1)}, f32[64,512]{1,0:T(8,128)S(1)}, bf16[512,1024]{1,0:T(8,128)(2,1)S(1)},...) custom-call(bf16[512,1024]{1,0:T(8,128)(2,1)} %bitcast.19, ...), custom_call_target="tpu_custom_call" | custom-call | flops 201326592 | bytes 16777216 | tf_op jit(solution)/shard_map/pallas_call | solution.py:53
  7.1 26.7 %all_to_all.25.mine = bf16[128,16,128]{2,1,0:T(8,128)(2,1)S(1)} all-to-all(bf16[128,16,128]{2,1,0:T(8,128)(2,1)S(1)} %get-tuple-element.28), channel_id=1, replica_groups={{154,218,26,90,158,222,30,94,130,194,2,66,134,198,6,70,138,202,10,74,14..., dimensions={0} | all-to-all | bytes 1048576 | tf_op jit(solution)/shard_map/all_to_all | solution.py:40
  33.8 0.0 collective-permute-done.up_other
  33.8 0.0 collective-permute-done.1.down_other
  33.8 4.7 %shard_map.85 = (bf16[128,16,128]{2,1,0:T(8,128)(2,1)S(1)}, bf16[2,128,1024]{2,1,0:T(8,128)(2,1)}, bf16[4,128,1024]{2,1,0:T(8,128)(2,1)}) custom-call(bf16[128,16,128]{2,1,0:T(8,128)(2,1)S(1)} %all_to_all.25.mine, bf16[1024,1024]{1,0:T(8,128)(2,1)S(1)} %get-tuple-element.29.up_own, bf16[1024,1024]{1,0:T(8,128)(2,1)S(1)} %collective-permute-done.up_other, ...), custom_call_target="tpu_custom_call" | custom-call | flops 2147483648 | bytes 4194304 | tf_op jit(solution)/shard_map/pallas_call | solution.py:53
  38.5 0.0 copy-start.1
  38.5 24.3 %all_to_all.26.returned = bf16[128,16,128]{2,1,0:T(8,128)(2,1)S(1)} all-to-all(bf16[128,16,128]{2,1,0:T(8,128)(2,1)S(1)} %get-tuple-element.31), channel_id=1, replica_groups={{154,218,26,90,158,222,30,94,130,194,2,66,134,198,6,70,138,202,10,74,14..., dimensions={0} | all-to-all | bytes 1048576 | tf_op jit(solution)/shard_map/all_to_all | solution.py:40
  62.9 0.0 copy-start
  62.9 0.0 copy-start.2
  62.9 1.1 %shard_map.86 = (bf16[64,512]{1,0:T(8,128)(2,1)S(1)}, bf16[64,1024]{1,0:T(8,128)(2,1)S(1)}, bf16[512,128]{1,0:T(8,128)(2,1)S(1)}) custom-call(bf16[128,16,128]{2,1,0:T(8,128)(2,1)S(1)} %all_to_all.26.returned, bf16[512,1024]{1,0:T(8,128)(2,1)S(1)} %get-tuple-element.32.tokens, bf16[512,1024]{1,0:T(8,128)(2,1)S(1)} %get-tuple-element.33.grads, ...), custom_call_target="tpu_custom_call" | custom-call | flops 201326592 | bytes 3145728 | tf_op jit(solution)/shard_map/pallas_call | solution.py:53
  64.0 13.6 %all_to_all.27.blocks = bf16[32,16,128]{2,1,0:T(8,128)(2,1)S(1)} all-to-all(bf16[32,16,128]{2,1,0:T(8,128)(2,1)S(1)} %bitcast.14), channel_id=1, replica_groups={{154,155,152,153,186,187,184,185,218,219,216,217,250,251,248,249,26,27,..., dimensions={0} | all-to-all | bytes 262144 | tf_op jit(solution)/shard_map/all_to_all | solution.py:40
  77.6 9.9 %all_to_all.28.blocks = f32[8,16,128]{2,1,0:T(8,128)S(1)} all-to-all(f32[8,16,128]{2,1,0:T(8,128)S(1)} %shard_map.87), channel_id=1, replica_groups={{154,158,130,134,138,142,146,150},{155,159,131,135,139,143,147,151},{15..., dimensions={0} | all-to-all | bytes 131072 | tf_op jit(solution)/shard_map/all_to_all | solution.py:40
  87.5 0.0 copy-done.1
  87.5 1.1 %collective-permute-start.2 = (bf16[4,128,1024]{2,1,0:T(8,128)(2,1)S(1)}, bf16[4,128,1024]{2,1,0:T(8,128)(2,1)S(1)}, u32[]{:S(2)}, u32[]{:S(2)}) collective-permute-start(bf16[4,128,1024]{2,1,0:T(8,128)(2,1)S(1)} %copy-done.1), channel_id=1, source_target_pairs={{0,1},{1,0},{2,3},{3,2},{4,5},{5,4},{6,7},{7,6},{8,9},{9,8},{10,11... | collective-permute-start | bytes 3145736 | tf_op jit(solution)/shard_map/ppermute | solution.py:30
  88.6 0.7 shard_map.88
  89.3 8.2 %all-to-all-start.4 = ((bf16[32,16,128]{2,1,0:T(8,128)(2,1)}), bf16[32,16,128]{2,1,0:T(8,128)(2,1)S(1)}, u32[]{:S(2)}, u32[]{:S(2)}) async-start(bf16[32,16,128]{2,1,0:T(8,128)(2,1)} %shard_map.88), calls=%async_computation.4 | async-start | bytes 262144 | tf_op jit(solution)/shard_map/all_to_all | solution.py:40
  97.5 0.0 copy-done
  97.5 1.4 %shard_map.89 = bf16[512,1024]{1,0:T(8,128)(2,1)} custom-call(f32[64,512]{1,0:T(8,128)S(1)} %get-tuple-element.34.dispatch, bf16[64,512]{1,0:T(8,128)(2,1)S(1)} %get-tuple-element.42.logit_grads, bf16[64,1024]{1,0:T(8,128)(2,1)S(1)} %get-tuple-element.43.slot_grads, bf16[64,1024]{1,0:T(8,128)(2,1)S(1)} %bitcast.12), custom_call_target="tpu_custom_call" | custom-call | flops 134217728 | bytes 2097152 | tf_op jit(solution)/shard_map/pallas_call | solution.py:53
  98.9 0.0 collective-permute-done.2.recv
  98.9 0.0 copy-done.2
  98.9 3.1 %shard_map.90 = (bf16[1024,1024]{1,0:T(8,128)(2,1)}, bf16[1024,1024]{1,0:T(8,128)(2,1)}) custom-call(bf16[2,128,1024]{2,1,0:T(8,128)(2,1)S(1)} %copy-done.2, bf16[4,128,1024]{2,1,0:T(8,128)(2,1)S(1)} %copy-done.1, bf16[4,128,1024]{2,1,0:T(8,128)(2,1)S(1)} %collective-permute-done.2.recv), custom_call_target="tpu_custom_call" | custom-call | flops 1073741824 | bytes 4194304 | tf_op jit(solution)/shard_map/pallas_call | solution.py:170
  102.0 0.0 all-to-all-done.4
  102.0 0.7 shard_map.91
  (1 shorter events, 0.0 us)
Async XLA Ops:
  0.6 33.2 %collective-permute-start = (bf16[1024,1024]{1,0:T(8,128)(2,1)}, bf16[1024,1024]{1,0:T(8,128)(2,1)S(1)}, u32[]{:S(2)}, u32[]{:S(2)}) collective-permute-start(bf16[1024,1024]{1,0:T(8,128)(2,1)} %bitcast.15), channel_id=1, source_target_pairs={{0,1},{1,0},{2,3},{3,2},{4,5},{5,4},{6,7},{7,6},{8,9},{9,8},{10,11... | collective-permute-start | bytes 6291464 | tf_op jit(solution)/shard_map/ppermute | solution.py:30
  4.0 29.8 %collective-permute-start.1 = (bf16[1024,1024]{1,0:T(8,128)(2,1)}, bf16[1024,1024]{1,0:T(8,128)(2,1)S(1)}, u32[]{:S(2)}, u32[]{:S(2)}) collective-permute-start(bf16[1024,1024]{1,0:T(8,128)(2,1)} %bitcast.17), channel_id=1, source_target_pairs={{0,1},{1,0},{2,3},{3,2},{4,5},{5,4},{6,7},{7,6},{8,9},{9,8},{10,11... | collective-permute-start | bytes 6291464 | tf_op jit(solution)/shard_map/ppermute | solution.py:30
  38.5 49.0 %copy-start.1 = (bf16[4,128,1024]{2,1,0:T(8,128)(2,1)S(1)}, bf16[4,128,1024]{2,1,0:T(8,128)(2,1)}, u32[]{:S(2)}) copy-start(bf16[4,128,1024]{2,1,0:T(8,128)(2,1)} %get-tuple-element.45.swap) | copy-start | bytes 3145732
  62.9 34.6 %copy-start = (bf16[1024,64]{0,1:T(8,128)(2,1)S(1)}, bf16[1024,64]{0,1:T(8,128)(2,1)}, u32[]{:S(2)}) copy-start(bf16[1024,64]{0,1:T(8,128)(2,1)} %param.6) | copy-start | bytes 393220
  62.9 36.0 %copy-start.2 = (bf16[2,128,1024]{2,1,0:T(8,128)(2,1)S(1)}, bf16[2,128,1024]{2,1,0:T(8,128)(2,1)}, u32[]{:S(2)}) copy-start(bf16[2,128,1024]{2,1,0:T(8,128)(2,1)} %get-tuple-element.44.keep) | copy-start | bytes 1572868
  87.5 11.4 %collective-permute-start.2 = (bf16[4,128,1024]{2,1,0:T(8,128)(2,1)S(1)}, bf16[4,128,1024]{2,1,0:T(8,128)(2,1)S(1)}, u32[]{:S(2)}, u32[]{:S(2)}) collective-permute-start(bf16[4,128,1024]{2,1,0:T(8,128)(2,1)S(1)} %copy-done.1), channel_id=1, source_target_pairs={{0,1},{1,0},{2,3},{3,2},{4,5},{5,4},{6,7},{7,6},{8,9},{9,8},{10,11... | collective-permute-start | bytes 3145736 | tf_op jit(solution)/shard_map/ppermute | solution.py:30
  89.3 12.7 %all-to-all-start.4 = ((bf16[32,16,128]{2,1,0:T(8,128)(2,1)}), bf16[32,16,128]{2,1,0:T(8,128)(2,1)S(1)}, u32[]{:S(2)}, u32[]{:S(2)}) async-start(bf16[32,16,128]{2,1,0:T(8,128)(2,1)} %shard_map.88), calls=%async_computation.4 | async-start | bytes 262144 | tf_op jit(solution)/shard_map/all_to_all | solution.py:40

commit v7 on v6

--- a/solution.py
+++ b/solution.py
@@ -282,15 +282,8 @@
     plane = lax.axis_size(PLANE)
     depth = lax.axis_size("z")
     blocks = exchange(blocks.reshape(plane, lines // plane, LANES), PLANE)
+    blocks, logit_grads, slot_grads = lax.optimization_barrier((blocks, logit_grads, slot_grads))
     (blocks,) = call(sum_kernel, [((depth, lines // plane, LANES), F32)])(blocks)
-    blocks = exchange(blocks, ("z",))
-    blocks, keep, swap, logit_grads, slot_grads = lax.optimization_barrier(
-        (blocks, keep, swap, logit_grads, slot_grads)
-    )
-    recv = swap_cores(swap)
-    (blocks,) = call(sum_kernel, [((plane, lines // plane, LANES), BF16)])(blocks)
-    blocks = exchange(blocks, PLANE).reshape(lines, LANES)
-    grad_up, grad_down = weight_grads(keep, swap, recv)
     (grad_image,) = call(
         image_kernel,
         [((count, width), BF16)],
@@ -298,7 +291,13 @@
         moved=4 * count * width,
         hbm_outs=None,
     )(dispatch, logit_grads, slot_grads, param)
-    blocks, grad_image, grad_up, grad_down = lax.optimization_barrier((blocks, grad_image, grad_up, grad_down))
+    blocks = exchange(blocks, ("z",))
+    blocks, grad_image, keep, swap = lax.optimization_barrier((blocks, grad_image, keep, swap))
+    recv = swap_cores(swap)
+    (blocks,) = call(sum_kernel, [((plane, lines // plane, LANES), BF16)])(blocks)
+    blocks = exchange(blocks, PLANE).reshape(lines, LANES)
+    grad_up, grad_down = weight_grads(keep, swap, recv)
+    blocks, grad_up, grad_down = lax.optimization_barrier((blocks, grad_up, grad_down))
     (param_grad,) = call(last_kernel, [((slots, width), F32)], hbm_outs=None)(blocks)
     return (grad_image[None], param_grad.T, grad_up[None], grad_down[None])
 

time: 103 us -> 103 us (level)
  blocking collectives: 74.5 us -> 64.6 us
  starting transfers between devices: 12.7 us -> 19.4 us
  waiting for transfers between devices: 0.01 us -> 2.75 us
    all_to_all x4 -> x3, blocking collectives: 74.5 us -> 64.6 us  [exchange(): lax.all_to_all(blocks, tuple(CUT), 0, 0, axis_index_groups=groups, tiled=...]
    all_to_all x1 -> x2, starting transfers between devices: 8.16 us -> 14.9 us  [exchange(): lax.all_to_all(blocks, tuple(CUT), 0, 0, axis_index_groups=groups, tiled=...]
    all_to_all x1 -> x2, waiting for transfers between devices: 0.01 us -> 2.74 us  [exchange(): lax.all_to_all(blocks, tuple(CUT), 0, 0, axis_index_groups=groups, tiled=...]
  transfers between devices with their start and end apart: 4 -> 5, of which waited for: 0 -> 1; matrix products, arithmetic and copies ran while one was open for 0% -> 0% of each run, Pallas kernels for 8% -> 8%
where the time goes in v7:
time: 103 us
  blocking collectives  64.6 us (63%)
  starting transfers between devices  19.4 us (19%)
  Pallas kernels  15.5 us (15%)
  waiting for transfers between devices  2.75 us (3%)
    all_to_all x3, blocking collectives, exchange(): lax.all_to_all(blocks, tuple(CUT), 0, 0, axis_index_groups=groups, tiled=...  64.6 us
    all_to_all x2, starting transfers between devices, exchange(): lax.all_to_all(blocks, tuple(CUT), 0, 0, axis_index_groups=groups, tiled=...  14.9 us
    pallas_call x7, Pallas kernels, run(): pl.pallas_call(kernel, out_shape=[shape_of(i, shape, dtype) for i, (shape...  12.4 us
    ppermute x3, starting transfers between devices, swap_cores(): return lax.ppermute(values, 'core', [(0, 1), (1, 0)])  4.53 us
    pallas_call x1, Pallas kernels, weight_grads(): pl.pallas_call(weights_kernel, grid=(width // step,), out_shape=[jax.Shap...  3.13 us
    all_to_all x2, waiting for transfers between devices, exchange(): lax.all_to_all(blocks, tuple(CUT), 0, 0, axis_index_groups=groups, tiled=...  2.74 us
  transfers between devices with their start and end apart: 5, of which 1 were waited for; matrix products, arithmetic and copies ran while one was open for 0% of the time, Pallas kernels for 8%

profile of v7, /device:TPU:1, one launch (start us, length us, event | category | flops | bytes accessed | tf_op | source)
XLA Modules:
  0.0 103.0 jit_solution(12999143220530039353)
XLA Ops:
  0.6 3.3 %collective-permute-start = (bf16[1024,1024]{1,0:T(8,128)(2,1)}, bf16[1024,1024]{1,0:T(8,128)(2,1)S(1)}, u32[]{:S(2)}, u32[]{:S(2)}) collective-permute-start(bf16[1024,1024]{1,0:T(8,128)(2,1)} %bitcast.15), channel_id=1, source_target_pairs={{0,1},{1,0},{2,3},{3,2},{4,5},{5,4},{6,7},{7,6},{8,9},{9,8},{10,11... | collective-permute-start | bytes 6291464 | tf_op jit(solution)/shard_map/ppermute | solution.py:30
  4.0 0.1 collective-permute-start.1
  4.1 3.0 %shard_map.84 = (bf16[128,16,128]{2,1,0:T(8,128)(2,1)S(1)}, f32[64,512]{1,0:T(8,128)S(1)}, f32[64,512]{1,0:T(8,128)S(1)}, bf16[512,1024]{1,0:T(8,128)(2,1)S(1)},...) custom-call(bf16[512,1024]{1,0:T(8,128)(2,1)} %bitcast.19, ...), custom_call_target="tpu_custom_call" | custom-call | flops 201326592 | bytes 16777216 | tf_op jit(solution)/shard_map/pallas_call | solution.py:53
  7.1 26.7 %all_to_all.25.mine = bf16[128,16,128]{2,1,0:T(8,128)(2,1)S(1)} all-to-all(bf16[128,16,128]{2,1,0:T(8,128)(2,1)S(1)} %get-tuple-element.29), channel_id=1, replica_groups={{154,218,26,90,158,222,30,94,130,194,2,66,134,198,6,70,138,202,10,74,14..., dimensions={0} | all-to-all | bytes 1048576 | tf_op jit(solution)/shard_map/all_to_all | solution.py:40
  33.8 0.0 collective-permute-done.up_other
  33.8 0.0 collective-permute-done.1.down_other
  33.8 4.7 %shard_map.85 = (bf16[128,16,128]{2,1,0:T(8,128)(2,1)S(1)}, bf16[2,128,1024]{2,1,0:T(8,128)(2,1)}, bf16[4,128,1024]{2,1,0:T(8,128)(2,1)}) custom-call(bf16[128,16,128]{2,1,0:T(8,128)(2,1)S(1)} %all_to_all.25.mine, bf16[1024,1024]{1,0:T(8,128)(2,1)S(1)} %get-tuple-element.30.up_own, bf16[1024,1024]{1,0:T(8,128)(2,1)S(1)} %collective-permute-done.up_other, ...), custom_call_target="tpu_custom_call" | custom-call | flops 2147483648 | bytes 4194304 | tf_op jit(solution)/shard_map/pallas_call | solution.py:53
  38.5 0.0 copy-start
  38.5 24.3 %all_to_all.26.returned = bf16[128,16,128]{2,1,0:T(8,128)(2,1)S(1)} all-to-all(bf16[128,16,128]{2,1,0:T(8,128)(2,1)S(1)} %get-tuple-element.32), channel_id=1, replica_groups={{154,218,26,90,158,222,30,94,130,194,2,66,134,198,6,70,138,202,10,74,14..., dimensions={0} | all-to-all | bytes 1048576 | tf_op jit(solution)/shard_map/all_to_all | solution.py:40
  62.9 0.0 copy-start.1
  62.9 0.0 copy-start.2
  62.9 1.1 %shard_map.86 = (bf16[64,512]{1,0:T(8,128)(2,1)S(1)}, bf16[64,1024]{1,0:T(8,128)(2,1)S(1)}, bf16[512,128]{1,0:T(8,128)(2,1)S(1)}) custom-call(bf16[128,16,128]{2,1,0:T(8,128)(2,1)S(1)} %all_to_all.26.returned, bf16[512,1024]{1,0:T(8,128)(2,1)S(1)} %get-tuple-element.33.tokens, bf16[512,1024]{1,0:T(8,128)(2,1)S(1)} %get-tuple-element.34.grads, ...), custom_call_target="tpu_custom_call" | custom-call | flops 201326592 | bytes 3145728 | tf_op jit(solution)/shard_map/pallas_call | solution.py:53
  64.0 13.6 %all_to_all.27.blocks = bf16[32,16,128]{2,1,0:T(8,128)(2,1)S(1)} all-to-all(bf16[32,16,128]{2,1,0:T(8,128)(2,1)S(1)} %bitcast.14), channel_id=1, replica_groups={{154,155,152,153,186,187,184,185,218,219,216,217,250,251,248,249,26,27,..., dimensions={0} | all-to-all | bytes 262144 | tf_op jit(solution)/shard_map/all_to_all | solution.py:40
  77.6 0.7 shard_map.87
  78.3 6.6 %all-to-all-start.3 = ((f32[8,16,128]{2,1,0:T(8,128)}), f32[8,16,128]{2,1,0:T(8,128)S(1)}, u32[]{:S(2)}, u32[]{:S(2)}) async-start(f32[8,16,128]{2,1,0:T(8,128)} %shard_map.87), calls=%async_computation.3 | async-start | bytes 131072 | tf_op jit(solution)/shard_map/all_to_all | solution.py:40
  84.9 0.0 copy-done
  84.9 1.4 %shard_map.88 = bf16[512,1024]{1,0:T(8,128)(2,1)} custom-call(f32[64,512]{1,0:T(8,128)S(1)} %get-tuple-element.35.dispatch, bf16[64,512]{1,0:T(8,128)(2,1)S(1)} %get-tuple-element.41.logit_grads, bf16[64,1024]{1,0:T(8,128)(2,1)S(1)} %get-tuple-element.42.slot_grads, bf16[64,1024]{1,0:T(8,128)(2,1)S(1)} %bitcast.12), custom_call_target="tpu_custom_call" | custom-call | flops 134217728 | bytes 2097152 | tf_op jit(solution)/shard_map/pallas_call | solution.py:53
  86.3 2.7 %all-to-all-done.3.blocks = f32[8,16,128]{2,1,0:T(8,128)S(1)} async-done(((f32[8,16,128]{2,1,0:T(8,128)}), f32[8,16,128]{2,1,0:T(8,128)S(1)}, u32[]{:S(2)}, u32[]{:S(2)}) %all-to-all-start.3) | async-done | bytes 65568 | tf_op jit(solution)/shard_map/all_to_all | solution.py:40
  89.0 0.0 copy-done.1
  89.0 1.1 %collective-permute-start.2 = (bf16[4,128,1024]{2,1,0:T(8,128)(2,1)S(1)}, bf16[4,128,1024]{2,1,0:T(8,128)(2,1)S(1)}, u32[]{:S(2)}, u32[]{:S(2)}) collective-permute-start(bf16[4,128,1024]{2,1,0:T(8,128)(2,1)S(1)} %copy-done.1), channel_id=1, source_target_pairs={{0,1},{1,0},{2,3},{3,2},{4,5},{5,4},{6,7},{7,6},{8,9},{9,8},{10,11... | collective-permute-start | bytes 3145736 | tf_op jit(solution)/shard_map/ppermute | solution.py:30
  90.1 0.7 shard_map.89
  90.8 8.3 %all-to-all-start.4 = ((bf16[32,16,128]{2,1,0:T(8,128)(2,1)}), bf16[32,16,128]{2,1,0:T(8,128)(2,1)S(1)}, u32[]{:S(2)}, u32[]{:S(2)}) async-start(bf16[32,16,128]{2,1,0:T(8,128)(2,1)} %shard_map.89), calls=%async_computation.4 | async-start | bytes 262144 | tf_op jit(solution)/shard_map/all_to_all | solution.py:40
  99.1 0.0 collective-permute-done.2.recv
  99.1 0.0 copy-done.2
  99.1 3.1 %shard_map.90 = (bf16[1024,1024]{1,0:T(8,128)(2,1)}, bf16[1024,1024]{1,0:T(8,128)(2,1)}) custom-call(bf16[2,128,1024]{2,1,0:T(8,128)(2,1)S(1)} %copy-done.2, bf16[4,128,1024]{2,1,0:T(8,128)(2,1)S(1)} %copy-done.1, bf16[4,128,1024]{2,1,0:T(8,128)(2,1)S(1)} %collective-permute-done.2.recv), custom_call_target="tpu_custom_call" | custom-call | flops 1073741824 | bytes 4194304 | tf_op jit(solution)/shard_map/pallas_call | solution.py:170
  102.3 0.0 all-to-all-done.4
  102.3 0.7 shard_map.91
Async XLA Ops:
  0.6 33.2 %collective-permute-start = (bf16[1024,1024]{1,0:T(8,128)(2,1)}, bf16[1024,1024]{1,0:T(8,128)(2,1)S(1)}, u32[]{:S(2)}, u32[]{:S(2)}) collective-permute-start(bf16[1024,1024]{1,0:T(8,128)(2,1)} %bitcast.15), channel_id=1, source_target_pairs={{0,1},{1,0},{2,3},{3,2},{4,5},{5,4},{6,7},{7,6},{8,9},{9,8},{10,11... | collective-permute-start | bytes 6291464 | tf_op jit(solution)/shard_map/ppermute | solution.py:30
  4.0 29.8 %collective-permute-start.1 = (bf16[1024,1024]{1,0:T(8,128)(2,1)}, bf16[1024,1024]{1,0:T(8,128)(2,1)S(1)}, u32[]{:S(2)}, u32[]{:S(2)}) collective-permute-start(bf16[1024,1024]{1,0:T(8,128)(2,1)} %bitcast.17), channel_id=1, source_target_pairs={{0,1},{1,0},{2,3},{3,2},{4,5},{5,4},{6,7},{7,6},{8,9},{9,8},{10,11... | collective-permute-start | bytes 6291464 | tf_op jit(solution)/shard_map/ppermute | solution.py:30
  38.5 46.3 %copy-start = (bf16[1024,64]{0,1:T(8,128)(2,1)S(1)}, bf16[1024,64]{0,1:T(8,128)(2,1)}, u32[]{:S(2)}) copy-start(bf16[1024,64]{0,1:T(8,128)(2,1)} %param.6) | copy-start | bytes 393220
  62.9 26.2 %copy-start.1 = (bf16[4,128,1024]{2,1,0:T(8,128)(2,1)S(1)}, bf16[4,128,1024]{2,1,0:T(8,128)(2,1)}, u32[]{:S(2)}) copy-start(bf16[4,128,1024]{2,1,0:T(8,128)(2,1)} %get-tuple-element.48.swap) | copy-start | bytes 3145732
  62.9 36.2 %copy-start.2 = (bf16[2,128,1024]{2,1,0:T(8,128)(2,1)S(1)}, bf16[2,128,1024]{2,1,0:T(8,128)(2,1)}, u32[]{:S(2)}) copy-start(bf16[2,128,1024]{2,1,0:T(8,128)(2,1)} %get-tuple-element.47.keep) | copy-start | bytes 1572868
  78.3 10.8 %all-to-all-start.3 = ((f32[8,16,128]{2,1,0:T(8,128)}), f32[8,16,128]{2,1,0:T(8,128)S(1)}, u32[]{:S(2)}, u32[]{:S(2)}) async-start(f32[8,16,128]{2,1,0:T(8,128)} %shard_map.87), calls=%async_computation.3 | async-start | bytes 131072 | tf_op jit(solution)/shard_map/all_to_all | solution.py:40
  89.0 10.1 %collective-permute-start.2 = (bf16[4,128,1024]{2,1,0:T(8,128)(2,1)S(1)}, bf16[4,128,1024]{2,1,0:T(8,128)(2,1)S(1)}, u32[]{:S(2)}, u32[]{:S(2)}) collective-permute-start(bf16[4,128,1024]{2,1,0:T(8,128)(2,1)S(1)} %copy-done.1), channel_id=1, source_target_pairs={{0,1},{1,0},{2,3},{3,2},{4,5},{5,4},{6,7},{7,6},{8,9},{9,8},{10,11... | collective-permute-start | bytes 3145736 | tf_op jit(solution)/shard_map/ppermute | solution.py:30
  90.8 11.4 %all-to-all-start.4 = ((bf16[32,16,128]{2,1,0:T(8,128)(2,1)}), bf16[32,16,128]{2,1,0:T(8,128)(2,1)S(1)}, u32[]{:S(2)}, u32[]{:S(2)}) async-start(bf16[32,16,128]{2,1,0:T(8,128)(2,1)} %shard_map.89), calls=%async_computation.4 | async-start | bytes 262144 | tf_op jit(solution)/shard_map/all_to_all | solution.py:40
